TPU v7x, 32 devices: a whole 2x2x4 slice. The times are simulated.
32 devices in a mesh: dp: 8 (over y, x, core), head: 4 (over z).
Axes of the slice: x: 2, y: 2, z: 4, core: 2. Of those that a mesh axis runs over, the one named last changes fastest.
Arguments:
- images: bfloat16 [160, 200, 768], P(('dp', 'head')), may hold values from -6 to 6
- mask_ids: int32 [160, 75], P(('dp', 'head')), may hold values from 1 to 196, as said below
- rel_index: int32 [200, 200], replicated, may hold values from 0 to 731, as said below
- out_grad: bfloat16 [160, 200, 768], P(('dp', 'head')), may hold values from -6 to 6
- mask_token: float32 [768], replicated, may hold values from -4 to 4
- attn_gain: float32 [768], replicated, may hold values from 0.5 to 1.5
- attn_shift: float32 [768], replicated, may hold values from -1.5 to 1.5
- qkv_weight: bfloat16 [3, 768, 768], P(None, None, 'head'), may hold values from -0.21875 to 0.21875
- qv_bias: float32 [2, 768], P(None, 'head'), may hold values from -1.5 to 1.5
- rel_table: float32 [732, 12], P(None, 'head'), may hold values from -4 to 4
- out_weight: bfloat16 [768, 768], P('head'), may hold values from -1.75 to 1.75
- out_bias: float32 [768], replicated, may hold values from -1.5 to 1.5
- attn_scale: float32 [768], replicated, may hold values from 0.5 to 1.5
- ffn_gain: float32 [768], replicated, may hold values from 0.5 to 1.5
- ffn_shift: float32 [768], replicated, may hold values from -1.5 to 1.5
- up_weight: bfloat16 [768, 3072], P(None, ('dp', 'head')), may hold values from -0.21875 to 0.21875
- up_bias: bfloat16 [3072], P(('dp', 'head')), may hold values from -1.5 to 1.5
- down_weight: bfloat16 [3072, 768], P(('dp', 'head')), may hold values from -0.109375 to 0.109375
- down_bias: float32 [768], replicated, may hold values from -1.5 to 1.5
- ffn_scale: float32 [768], replicated, may hold values from 0.5 to 1.5
Outputs:
- output: bfloat16 [160, 200, 768], P(('dp', 'head'))
- images_grad: bfloat16 [160, 200, 768], P(('dp', 'head'))
- mask_token_grad: float32 [768], replicated
- attn_gain_grad: float32 [768], replicated
- attn_shift_grad: float32 [768], replicated
- qkv_weight_grad: float32 [3, 768, 768], P(None, None, 'head')
- qv_bias_grad: float32 [2, 768], P(None, 'head')
- rel_table_grad: float32 [732, 12], P(None, 'head')
- out_weight_grad: float32 [768, 768], P('head')
- out_bias_grad: float32 [768], replicated
- attn_scale_grad: float32 [768], replicated
- ffn_gain_grad: float32 [768], replicated
- ffn_shift_grad: float32 [768], replicated
- up_weight_grad: float32 [768, 3072], P(None, ('dp', 'head'))
- up_bias_grad: float32 [3072], P(('dp', 'head'))
- down_weight_grad: float32 [3072, 768], P(('dp', 'head'))
- down_bias_grad: float32 [768], replicated
- ffn_scale_grad: float32 [768], replicated
Inputs may be any that keep to these rules, and one draw needn't show every extreme that they name: `mask_ids`: each image's 75 ids are distinct patch positions, from 1 to 196. Rows and columns 1 to 196 stand for the patches of a 14 by 14 grid in some order, and there rel_index[q, k] = (dy + 13) * 27 + dx + 13 with (dy, dx) the grid offset of q's patch from k's; row 0 holds 729, column 0 below it 732 - 2, entry [0, 0] holds 731; entries of padding rows and columns are any table rows.
All inputs are finite; a program needn't handle non-finite values.
Results may differ from a plain program's by a relative error of at most 0.015.
Values may be sent and summed in bfloat16 or wider, within the bound.
No kernel may reach another device: no remote copies, remote signals or barrier semaphores. Data moves between devices by JAX's collectives and lax.ppermute only.
A program may use at most 192 MiB of HBM per device.

v0:
```python
from functools import partial

import jax
import jax.numpy as jnp
from jax import lax
from jax.sharding import PartitionSpec as P

HEAD_DIM = 64
SEQ = 200
VALID = 197


EPS = 1e-06
NEG = -1000000000.0


def norm_stats(rows):
    row_mean = jnp.mean(rows, axis=-1, keepdims=True)
    centered = rows - row_mean
    inv_std = lax.rsqrt(jnp.mean(centered * centered, axis=-1, keepdims=True) + EPS)
    return (centered * inv_std, inv_std)


def norm_back(grad_normed, normal, inv_std, gain):
    scaled = grad_normed * gain
    return inv_std * (
        scaled
        - jnp.mean(scaled, axis=-1, keepdims=True)
        - normal * jnp.mean(scaled * normal, axis=-1, keepdims=True)
    )


def exact_gelu(values):
    return jax.nn.gelu(values, approximate=False)


def gelu_back(pre_act, grad_act):
    return jax.vjp(exact_gelu, pre_act)[1](grad_act)[0]


def relative_bias(rel_index, rel_table):
    picked = jnp.take(rel_table, rel_index.reshape(-1), axis=0)
    return picked.T.reshape(rel_table.shape[1], SEQ, SEQ)


def table_grad(rel_index, grad_bias, table_rows):
    heads_here = grad_bias.shape[0]
    flat_grad = grad_bias.reshape(heads_here, -1).T
    start = jnp.zeros((table_rows, heads_here), jnp.float32)
    return start.at[rel_index.reshape(-1)].add(flat_grad)


def masked_scores(queries, key_vecs, rel_bias, keep):
    scores = (
        jnp.einsum("bqhd,bkhd->bhqk", queries, key_vecs, preferred_element_type=jnp.float32)
        + rel_bias[None]
    )
    return jnp.where(keep, scores, NEG)


def attend_forward(rel_bias, keep, block_data):
    queries, key_vecs, values_in = block_data
    scores = masked_scores(queries, key_vecs, rel_bias, keep)
    row_max = jnp.max(scores, axis=-1, keepdims=True)
    row_exp = jnp.exp(scores - row_max)
    row_total = jnp.sum(row_exp, axis=-1, keepdims=True)
    attn_probs = (row_exp / row_total).astype(jnp.bfloat16)
    attended = jnp.einsum(
        "bhqk,bkhd->bqhd", attn_probs, values_in, preferred_element_type=jnp.float32
    )
    log_total = row_max[..., 0] + jnp.log(row_total[..., 0])
    return (attended.astype(jnp.bfloat16), log_total)


def attend_backward(rel_bias, keep, block_data):
    queries, key_vecs, values_in, grad_att, log_total = block_data
    scores = masked_scores(queries, key_vecs, rel_bias, keep)
    soft = jnp.exp(scores - log_total[..., None])
    attn_probs = soft.astype(jnp.bfloat16)
    grad_vals = jnp.einsum(
        "bhqk,bqhd->bkhd", attn_probs, grad_att, preferred_element_type=jnp.float32
    )
    grad_probs = jnp.einsum(
        "bqhd,bkhd->bhqk", grad_att, values_in, preferred_element_type=jnp.float32
    )
    centre = jnp.sum(soft * grad_probs, axis=-1, keepdims=True)
    grad_scores = (soft * (grad_probs - centre)).astype(jnp.bfloat16)
    grad_queries = jnp.einsum(
        "bhqk,bkhd->bqhd", grad_scores, key_vecs, preferred_element_type=jnp.float32
    )
    grad_keys = jnp.einsum(
        "bhqk,bqhd->bkhd", grad_scores, queries, preferred_element_type=jnp.float32
    )
    grad_bias = jnp.sum(grad_scores.astype(jnp.float32), axis=0)
    return (
        grad_queries.astype(jnp.bfloat16),
        grad_keys.astype(jnp.bfloat16),
        grad_vals.astype(jnp.bfloat16),
        grad_bias,
    )


def on_device(
    images,
    mask_ids,
    rel_index,
    out_grad,
    mask_token,
    attn_gain,
    attn_shift,
    qkv_weight,
    qv_bias,
    rel_table,
    out_weight,
    out_bias,
    attn_scale,
    ffn_gain,
    ffn_shift,
    up_weight,
    up_bias,
    down_weight,
    down_bias,
    ffn_scale,
):
    count_img, seq_rows, width = images.shape
    scale_q = HEAD_DIM ** (-0.5)
    positions = jnp.arange(SEQ, dtype=jnp.int32)
    masked = jnp.any(mask_ids[:, :, None] == positions[None, None, :], axis=1)[:, :, None]
    keep = positions < VALID
    hidden = jnp.where(masked, mask_token, images.astype(jnp.float32))
    normal_one, inv_one = norm_stats(hidden)
    normed_one = (normal_one * attn_gain + attn_shift).astype(jnp.bfloat16)
    qkv_all, out_all, qv_all, table_all = (qkv_weight, out_weight, qv_bias, rel_table)
    rows_full = lax.all_gather(normed_one, "head", axis=0, tiled=True)
    heads_here = table_all.shape[1]
    inner_width = heads_here * HEAD_DIM
    group_img = rows_full.shape[0]
    per_block = max(
        (divisor for divisor in range(1, min(group_img, 4) + 1) if group_img % divisor == 0)
    )
    block_count = group_img // per_block

    def to_blocks(array):
        return array.reshape(block_count, per_block, SEQ, heads_here, HEAD_DIM)

    def from_blocks(array):
        return array.reshape(group_img, SEQ, inner_width)

    projected = jnp.einsum("bsd,jde->jbse", rows_full, qkv_all, preferred_element_type=jnp.float32)
    queries = ((projected[0] + qv_all[0]) * scale_q).astype(jnp.bfloat16)
    key_vecs = projected[1].astype(jnp.bfloat16)
    values_in = (projected[2] + qv_all[1]).astype(jnp.bfloat16)
    rel_bias = relative_bias(rel_index, table_all)
    attended_blocks, log_total = lax.map(
        partial(attend_forward, rel_bias, keep),
        (to_blocks(queries), to_blocks(key_vecs), to_blocks(values_in)),
    )
    attended = from_blocks(attended_blocks)
    out_partial = jnp.einsum("bse,ed->bsd", attended, out_all, preferred_element_type=jnp.float32)
    branch = lax.psum_scatter(out_partial, "head", scatter_dimension=0, tiled=True) + out_bias
    middle = hidden + attn_scale * branch
    normal_two, inv_two = norm_stats(middle)
    normed_two = (normal_two * ffn_gain + ffn_shift).astype(jnp.bfloat16)
    up_full, up_bias_full, down_full = (
        lax.all_gather(up_weight, ("dp", "head"), axis=1, tiled=True),
        lax.all_gather(up_bias, ("dp", "head"), axis=0, tiled=True),
        lax.all_gather(down_weight, ("dp", "head"), axis=0, tiled=True),
    )
    flat_two = normed_two.reshape(-1, width)
    pre_act = jnp.dot(flat_two, up_full, preferred_element_type=jnp.float32) + up_bias_full.astype(
        jnp.float32
    )
    activated = exact_gelu(pre_act).astype(jnp.bfloat16)
    mlp_flat = jnp.dot(activated, down_full, preferred_element_type=jnp.float32) + down_bias
    mlp_out = mlp_flat.reshape(count_img, seq_rows, width)
    output = (middle + ffn_scale * mlp_out).astype(jnp.bfloat16)
    grad_output = out_grad.astype(jnp.float32)
    grad_ffn_scale = jnp.sum(grad_output * mlp_out, axis=(0, 1))
    grad_mlp = (grad_output * ffn_scale).astype(jnp.bfloat16)
    grad_down_bias = jnp.sum(grad_mlp.astype(jnp.float32), axis=(0, 1))
    grad_mlp_flat = grad_mlp.reshape(-1, width)
    grad_down = jnp.einsum(
        "rf,rd->fd", activated, grad_mlp_flat, preferred_element_type=jnp.float32
    )
    grad_act = jnp.einsum("rd,fd->rf", grad_mlp_flat, down_full, preferred_element_type=jnp.float32)
    grad_pre = gelu_back(pre_act, grad_act).astype(jnp.bfloat16)
    grad_up = jnp.einsum("rd,rf->df", flat_two, grad_pre, preferred_element_type=jnp.float32)
    grad_up_bias = jnp.sum(grad_pre.astype(jnp.float32), axis=0)
    grad_normed_two = jnp.einsum(
        "rf,df->rd", grad_pre, up_full, preferred_element_type=jnp.float32
    ).reshape(count_img, seq_rows, width)
    up_weight_grad, up_bias_grad, down_weight_grad = (
        lax.psum_scatter(grad_up, ("dp", "head"), scatter_dimension=1, tiled=True),
        lax.psum_scatter(grad_up_bias, ("dp", "head"), scatter_dimension=0, tiled=True),
        lax.psum_scatter(grad_down, ("dp", "head"), scatter_dimension=0, tiled=True),
    )
    grad_ffn_gain = jnp.sum(grad_normed_two * normal_two, axis=(0, 1))
    grad_ffn_shift = jnp.sum(grad_normed_two, axis=(0, 1))
    grad_middle = grad_output + norm_back(grad_normed_two, normal_two, inv_two, ffn_gain)
    grad_attn_scale = jnp.sum(grad_middle * branch, axis=(0, 1))
    grad_branch = (grad_middle * attn_scale).astype(jnp.bfloat16)
    grad_out_bias = jnp.sum(grad_branch.astype(jnp.float32), axis=(0, 1))
    branch_rows = lax.all_gather(grad_branch, "head", axis=0, tiled=True)
    grad_out_w = jnp.einsum(
        "bse,bsd->ed", attended, branch_rows, preferred_element_type=jnp.float32
    )
    grad_attended = jnp.einsum(
        "bsd,ed->bse", branch_rows, out_all, preferred_element_type=jnp.float32
    ).astype(jnp.bfloat16)
    grad_q_blocks, grad_k_blocks, grad_v_blocks, grad_bias_blocks = lax.map(
        partial(attend_backward, rel_bias, keep),
        (
            to_blocks(queries),
            to_blocks(key_vecs),
            to_blocks(values_in),
            to_blocks(grad_attended),
            log_total,
        ),
    )
    grad_bias = jnp.sum(grad_bias_blocks, axis=0)
    grad_table = table_grad(rel_index, grad_bias, table_all.shape[0])
    grad_proj = jnp.stack(
        [
            from_blocks(grad_q_blocks) * scale_q,
            from_blocks(grad_k_blocks),
            from_blocks(grad_v_blocks),
        ]
    )
    grad_qv_bias = jnp.stack(
        [
            jnp.sum(grad_proj[0].astype(jnp.float32), axis=(0, 1)),
            jnp.sum(grad_proj[2].astype(jnp.float32), axis=(0, 1)),
        ]
    )
    grad_qkv = jnp.einsum("bsd,jbse->jde", rows_full, grad_proj, preferred_element_type=jnp.float32)
    normed_one_terms = jnp.einsum(
        "jbse,jde->bsd", grad_proj, qkv_all, preferred_element_type=jnp.float32
    )
    grad_normed_one = lax.psum_scatter(
        normed_one_terms.astype(jnp.bfloat16), "head", scatter_dimension=0, tiled=True
    ).astype(jnp.float32)
    grad_attn_gain = jnp.sum(grad_normed_one * normal_one, axis=(0, 1))
    grad_attn_shift = jnp.sum(grad_normed_one, axis=(0, 1))
    grad_hidden = grad_middle + norm_back(grad_normed_one, normal_one, inv_one, attn_gain)
    images_grad = jnp.where(masked, 0.0, grad_hidden).astype(jnp.bfloat16)
    grad_mask_token = jnp.sum(jnp.where(masked, grad_hidden, 0.0), axis=(0, 1))
    qkv_weight_grad, qv_bias_grad, rel_table_grad, out_weight_grad = lax.psum(
        (grad_qkv, grad_qv_bias, grad_table, grad_out_w), "dp"
    )
    (
        mask_token_grad,
        attn_gain_grad,
        attn_shift_grad,
        out_bias_grad,
        attn_scale_grad,
        ffn_gain_grad,
        ffn_shift_grad,
        down_bias_grad,
        ffn_scale_grad,
    ) = lax.psum(
        (
            grad_mask_token,
            grad_attn_gain,
            grad_attn_shift,
            grad_out_bias,
            grad_attn_scale,
            grad_ffn_gain,
            grad_ffn_shift,
            grad_down_bias,
            grad_ffn_scale,
        ),
        ("dp", "head"),
    )
    return (
        output,
        images_grad,
        mask_token_grad,
        attn_gain_grad,
        attn_shift_grad,
        qkv_weight_grad,
        qv_bias_grad,
        rel_table_grad,
        out_weight_grad,
        out_bias_grad,
        attn_scale_grad,
        ffn_gain_grad,
        ffn_shift_grad,
        up_weight_grad,
        up_bias_grad,
        down_weight_grad,
        down_bias_grad,
        ffn_scale_grad,
    )


def solution(mesh):
    in_specs = (
        P(("dp", "head"), None, None),
        P(("dp", "head"), None),
        P(),
        P(("dp", "head"), None, None),
        P(),
        P(),
        P(),
        P(None, None, "head"),
        P(None, "head"),
        P(None, "head"),
        P("head", None),
        P(),
        P(),
        P(),
        P(),
        P(None, ("dp", "head")),
        P(("dp", "head")),
        P(("dp", "head"), None),
        P(),
        P(),
    )
    out_specs = (
        P(("dp", "head"), None, None),
        P(("dp", "head"), None, None),
        P(),
        P(),
        P(),
        P(None, None, "head"),
        P(None, "head"),
        P(None, "head"),
        P("head", None),
        P(),
        P(),
        P(),
        P(),
        P(None, ("dp", "head")),
        P(("dp", "head")),
        P(("dp", "head"), None),
        P(),
        P(),
    )
    return jax.shard_map(
        on_device, mesh=mesh, in_specs=in_specs, out_specs=out_specs, check_vma=False
    )
```

profile of v0, /device:TPU:0, one launch (start us, length us, event | category | flops | bytes accessed | tf_op | source)
XLA Modules:
  0.0 1180.2 jit_solution(13923624107879108132)
XLA Ops:
  17.5 74.2 %gather_fusion = f32[40000,3]{1,0:T(8,128)} fusion(f32[732,3]{1,0:T(8,128)S(1)} %copy.68, s32[40960]{0:T(1024)S(1)} %pad_clamp_fusion), kind=kCustom, calls=%fused_computation | custom fusion | bytes 1120000 | tf_op jit(solution)/shard_map/jit(_take)/gather | solution.py:42
  91.7 22.6 %select_bitcast_fusion = f32[3,40000]{0,1:T(8,128)} fusion(f32[40000,3]{1,0:T(8,128)} %gather_fusion, pred[40000]{0:T(1024)(128)(4,1)S(1)} %compare_and_fusion), kind=kLoop, calls=%fused_computation.61 | loop fusion | flops 120000 | bytes 1000000 | tf_op jit(solution)/shard_map/jit(_take)/select_n | solution.py:42
  114.3 11.7 copy.69
  131.0 6.8 fusion.62
  140.3 3.0 multiply_convert_fusion.2
  144.9 35.4 %while.32 = (s32[]{:T(128)}, bf16[5,4,200,3,64]{2,4,3,1,0:T(8,128)(2,1)}, f32[5,4,3,200]{3,2,1,0:T(4,128)}, bf16[5,4,200,3,64]{2,4,3,1,0:T(8,128)(2,1)}, bf16[5,...) while((s32[]{:T(128)}, ...), condition=%wide.wide.region_6.7_spmd.clone, body=%wide.wide.region_3.0_spmd.clone.sunk | while | flops 128791400 | bytes 9819401 | solution.py:154
  180.3 7.9 fusion.82
  189.8 48.2 %all-reduce = bf16[3072]{0:T(1024)(128)(2,1)S(1)} all-reduce(bf16[3072]{0:T(1024)(128)(2,1)S(1)} %dynamic-update-slice), channel_id=1, replica_groups=mesh['dp'=8,'head'=4] {'dp','head'}, use_global_device_ids=true, to_apply=%add | all-reduce | flops 3072 | bytes 12288
  238.0 3.5 convert_reduce_fusion.5
  241.5 163.6 %reduce-scatter.5.cloned.1.call-done = f32[5,200,768]{2,1,0:T(8,128)} async-done(((f32[20,200,768]{2,1,0:T(8,128)}), f32[5,200,768]{2,1,0:T(8,128)}) %reduce-scatter.5.cloned.1.call-update) | async-done | bytes 3072016 | tf_op jit(solution)/shard_map/reduce_scatter | solution.py:160
  411.8 20.2 %all-gather.7.cloned.1.call-done = bf16[768,3072]{0,1:T(8,128)(2,1)} async-done(((bf16[768,96]{0,1:T(8,128)(2,1)}), bf16[768,3072]{0,1:T(8,128)(2,1)}) %all-gather.7.cloned.1.call-update) | async-done | bytes 4718608 | tf_op jit(solution)/shard_map/all_gather | solution.py:165
  432.0 12.4 %fusion.94 = f32[1000,3072]{1,0:T(8,128)} fusion(bf16[1000,768]{1,0:T(8,128)(2,1)} %bitcast.207, bf16[768,3072]{0,1:T(8,128)(2,1)} %all-gather.7.cloned.1.call-done), kind=kOutput, calls=%fused_computation.163 | convolution fusion | flops 4718592000 | bytes 18542592 | tf_op jit(solution)/shard_map/dot_general | solution.py:170
  444.4 52.4 %all-gather.9.cloned.1.call-done = bf16[3072,768]{1,0:T(8,128)(2,1)} async-done(((bf16[96,768]{1,0:T(8,128)(2,1)}), bf16[3072,768]{1,0:T(8,128)(2,1)}) %all-gather.9.cloned.1.call-update) | async-done | bytes 4718608 | tf_op jit(solution)/shard_map/all_gather | solution.py:167
  496.8 36.0 %convert_reduce_fusion.1 = (f32[3072]{0:T(1024)S(1)}, bf16[1000,3072]{1,0:T(8,128)(2,1)S(1)}, f32[1000,3072]{1,0:T(8,128)S(1)}) fusion(f32[1000,3072]{1,0:T(8,128)} %fusion.94, f32[3072]{0:T(1024)S(1)} %convert_element_type.114, bf16[1000,768]{1,0:T(8,128)(2,1)S(1)} %bitcast.205, bf16[3072,768]{1,0:T(8,128)(2,1)} %all-gather.9.cloned.1.call-done), kind=kOutput, calls=%fused_computation.65 | convolution fusion | flops 4948988928 | bytes 36999168 | tf_op jit(solution)/shard_map/rd,fd->rf/dot_general | solution.py:185
  532.8 12.1 %multiply_convert_fusion.1 = bf16[1000,3072]{1,0:T(8,128)(2,1)} fusion(f32[1000,3072]{1,0:T(8,128)S(1)} %get-tuple-element.348, f32[1000,3072]{1,0:T(8,128)} %fusion.94, f32[3072]{0:T(1024)S(1)} %convert_element_type.114), kind=kLoop, calls=%fused_computation.67 | loop fusion | flops 12288000 | bytes 30732288 | tf_op jit(solution)/shard_map/convert_element_type | solution.py:173
  545.0 5.1 fusion.89
  551.9 8.6 convolution_add_fusion
  560.6 3.9 fusion.70
  566.3 109.5 %all-gather.11.cloned.1.call-done = bf16[20,200,768]{2,1,0:T(8,128)(2,1)} async-done(((bf16[5,200,768]{2,1,0:T(8,128)(2,1)}), bf16[20,200,768]{2,1,0:T(8,128)(2,1)}) %all-gather.11.cloned.1.call-update) | async-done | bytes 6144016 | tf_op jit(solution)/shard_map/all_gather | solution.py:203
  675.8 5.8 convolution_convert_fusion.4
  686.3 79.6 %while.33 = (s32[]{:T(128)}, bf16[5,4,200,3,64]{2,4,3,1,0:T(8,128)(2,1)}, bf16[5,4,200,3,64]{2,4,3,1,0:T(8,128)(2,1)}, bf16[5,4,200,3,64]{2,4,3,1,0:T(8,128)(2,1...) while((s32[]{:T(128)}, ...), condition=%wide.wide.region_15.16_spmd.clone, body=%wide.wide.region_12.15_spmd.clone.sunk | while | flops 312818592 | bytes 24414648 | solution.py:210
  769.1 7.1 bitcast_convert_fusion
  777.7 5.3 convolution_bitcast_fusion
  783.6 8.6 fusion.75
  792.2 12.5 %fusion.95 = f32[768,3072]{0,1:T(8,128)} fusion(bf16[1000,768]{1,0:T(8,128)(2,1)S(1)} %bitcast.208, bf16[1000,3072]{1,0:T(8,128)(2,1)} %copy-done.58), kind=kOutput, calls=%fused_computation.164 | convolution fusion | flops 4718592000 | bytes 17117184 | tf_op jit(solution)/shard_map/rd,rf->df/dot_general | solution.py:187
  806.2 10.6 fusion.96
  821.9 10.7 copy.80
  832.6 216.0 %scatter_custom_fusion = f32[732,3]{1,0:T(8,128)S(1)} fusion(s32[40000]{0:T(1024)} %copy-done.24, f32[40000,3]{1,0:T(8,128)} %bitcast.190, f32[]{:T(128)} %constant.37.clone.1), kind=kCustom, calls=%fused_computation.142 | custom fusion | flops 120000 | bytes 9296 | tf_op jit(solution)/shard_map/scatter-add | solution.py:50
  1048.6 28.7 %all-reduce.3 = (f32[2,192]{1,0:T(2,128)}, f32[732,3]{1,0:T(8,128)S(1)}) all-reduce(f32[2,192]{1,0:T(2,128)S(1)} %pad_maximum_fusion.5, f32[732,3]{1,0:T(8,128)S(1)} %scatter_custom_fusion), channel_id=1, replica_groups=mesh['dp'=8,'head'=4] {'dp'}, use_global_device_ids=true, to_apply=%region_28.29 | all-reduce | flops 2580 | bytes 20640 | tf_op jit(solution)/shard_map/psum | solution.py:247
  1081.0 5.9 fusion.71
  1086.8 40.5 %all-reduce.2 = (f32[768]{0:T(1024)}, f32[768]{0:T(1024)}, f32[768]{0:T(1024)}, f32[768]{0:T(1024)}, f32[768]{0:T(1024)}, /*index=5*/f32[768]{0:T(1024)}, f32[76...) all-reduce(f32[768]{0:T(1024)S(1)} %get-tuple-element.283, ...), channel_id=1, replica_groups=mesh['dp'=8,'head'=4] {'dp','head'}, use_global_device_ids=true, to_apply=%region_20.21 | all-reduce | flops 9984 | bytes 79872 | tf_op jit(solution)/shard_map/psum | solution.py:260
  1127.9 40.7 %reduce-scatter.11.cloned.1.call-done = f32[96,768]{1,0:T(8,128)} async-done(((f32[3072,768]{1,0:T(8,128)}), f32[96,768]{1,0:T(8,128)}) %reduce-scatter.11.cloned.1.call-update) | async-done | bytes 294928 | tf_op jit(solution)/shard_map/reduce_scatter | solution.py:195
  (284 shorter events, 168.6 us)
Async XLA Ops:
  8.0 123.0 %copy-start = (bf16[3,768,192]{1,2,0:T(8,128)(2,1)S(1)}, bf16[3,768,192]{1,2,0:T(8,128)(2,1)}, u32[]{:S(2)}) copy-start(bf16[3,768,192]{1,2,0:T(8,128)(2,1)} %param.31) | copy-start | bytes 2654212
  8.1 122.9 %all-gather.5.cloned.1.call-start = ((), (), s32[]{:S(2)}) async-start(), calls=%async_computation.4 | async-start | bytes 7680000 | tf_op jit(solution)/shard_map/all_gather | solution.py:134
  9.1 396.1 %copy-start.38 = (pred[5,200]{1,0:T(8,128)(4,1)}, pred[5,200]{1,0:T(8,128)(4,1)S(1)}, u32[]{:S(2)}) copy-start(pred[5,200]{1,0:T(8,128)(4,1)S(1)} %fusion.80) | copy-start | bytes 3004
  15.2 389.9 %reduce-scatter.5.cloned.1.call-start = ((), (), s32[]{:S(2)}) async-start(), calls=%async_computation.5 | async-start | bytes 15360000 | tf_op jit(solution)/shard_map/reduce_scatter | solution.py:160
  144.9 35.4 %copy-start.26 = (bf16[192,768]{1,0:T(8,128)(2,1)S(1)}, bf16[192,768]{1,0:T(8,128)(2,1)}, u32[]{:S(2)}) copy-start(bf16[192,768]{1,0:T(8,128)(2,1)} %param.34) | copy-start | bytes 884740
  188.2 49.7 %copy-start.49 = (f32[768]{0:T(1024)S(1)}, f32[768]{0:T(1024)}, u32[]{:S(2)}) copy-start(f32[768]{0:T(1024)} %param.43) | copy-start | bytes 9220
  188.3 216.9 %copy-start.44 = (f32[768]{0:T(1024)S(1)}, f32[768]{0:T(1024)}, u32[]{:S(2)}) copy-start(f32[768]{0:T(1024)} %param.35) | copy-start | bytes 9220
  188.3 216.9 %copy-start.47 = (f32[768]{0:T(1024)S(1)}, f32[768]{0:T(1024)}, u32[]{:S(2)}) copy-start(f32[768]{0:T(1024)} %param.36) | copy-start | bytes 9220
  188.3 243.7 %all-gather.7.cloned.1.call-start = ((), (), s32[]{:S(2)}) async-start(), calls=%async_computation.6 | async-start | bytes 4866048 | tf_op jit(solution)/shard_map/all_gather | solution.py:165
  188.9 307.9 %all-gather.9.cloned.1.call-start = ((), (), s32[]{:S(2)}) async-start(), calls=%async_computation.7 | async-start | bytes 4866048 | tf_op jit(solution)/shard_map/all_gather | solution.py:167
  189.4 486.4 %all-gather.11.cloned.1.call-start = ((), (), s32[]{:S(2)}) async-start(), calls=%async_computation.8 | async-start | bytes 7680000 | tf_op jit(solution)/shard_map/all_gather | solution.py:203
  432.0 64.8 %copy-start.20 = (bf16[5,200,768]{2,1,0:T(8,128)(2,1)S(1)}, bf16[5,200,768]{2,1,0:T(8,128)(2,1)}, u32[]{:S(2)}) copy-start(bf16[5,200,768]{2,1,0:T(8,128)(2,1)} %get-tuple-element.345) | copy-start | bytes 4608004
  532.8 12.2 %copy-start.58 = (bf16[1000,3072]{1,0:T(8,128)(2,1)}, bf16[1000,3072]{1,0:T(8,128)(2,1)S(1)}, u32[]{:S(2)}) copy-start(bf16[1000,3072]{1,0:T(8,128)(2,1)S(1)} %get-tuple-element.347) | copy-start | bytes 18432004
  532.8 12.2 %copy-start.43 = (f32[768]{0:T(1024)S(1)}, f32[768]{0:T(1024)}, u32[]{:S(2)}) copy-start(f32[768]{0:T(1024)} %param.37) | copy-start | bytes 9220
  532.8 12.2 %copy-start.55 = (bf16[768,3072]{0,1:T(8,128)(2,1)S(1)}, bf16[768,3072]{0,1:T(8,128)(2,1)}, u32[]{:S(2)}) copy-start(bf16[768,3072]{0,1:T(8,128)(2,1)} %all-gather.7.cloned.1.call-done) | copy-start | bytes 14155780
  551.8 8.7 copy-start.3
  551.9 8.7 copy-start.9
  551.9 8.7 copy-start.14
  551.9 8.7 copy-start.48
  560.6 115.2 %copy-start.27 = (bf16[192,768]{1,0:T(8,128)(2,1)S(1)}, bf16[192,768]{1,0:T(8,128)(2,1)}, u32[]{:S(2)}) copy-start(bf16[192,768]{1,0:T(8,128)(2,1)} %param.34) | copy-start | bytes 884740
  564.5 513.6 %reduce-scatter.7.cloned.1.call-start = ((), (), s32[]{:S(2)}) async-start(), calls=%async_computation.9 | async-start | bytes 7680000 | tf_op jit(solution)/shard_map/reduce_scatter | solution.py:239
  776.2 351.7 %all-reduce.7.cloned.1.call-start = ((), (), s32[]{:S(2)}) async-start(), calls=%async_computation.12 | async-start | bytes 4718592 | tf_op jit(solution)/shard_map/psum | solution.py:247
  792.2 335.7 %reduce-scatter.9.cloned.1.call-start = ((), (), s32[]{:S(2)}) async-start(), calls=%async_computation.10 | async-start | bytes 9732096 | tf_op jit(solution)/shard_map/reduce_scatter | solution.py:193
  804.8 363.8 %reduce-scatter.11.cloned.1.call-start = ((), (), s32[]{:S(2)}) async-start(), calls=%async_computation.11 | async-start | bytes 9732096 | tf_op jit(solution)/shard_map/reduce_scatter | solution.py:195
  821.8 256.2 %copy-start.6 = (bf16[5,200,768]{2,1,0:T(8,128)(2,1)S(1)}, bf16[5,200,768]{2,1,0:T(8,128)(2,1)}, u32[]{:S(2)}) copy-start(bf16[5,200,768]{2,1,0:T(8,128)(2,1)} %param.24) | copy-start | bytes 4608004
  821.9 256.2 %copy-start.31 = (f32[5,200]{1,0:T(8,128)S(1)}, f32[5,200]{1,0:T(8,128)}, u32[]{:S(2)}) copy-start(f32[5,200]{1,0:T(8,128)} %copy-done.30) | copy-start | bytes 12004
  821.9 256.2 %copy-start.33 = (f32[768]{0:T(1024)S(1)}, f32[768]{0:T(1024)}, u32[]{:S(2)}) copy-start(f32[768]{0:T(1024)} %param.28) | copy-start | bytes 9220
  821.9 256.2 %copy-start.37 = (f32[5,200]{1,0:T(8,128)S(1)}, f32[5,200]{1,0:T(8,128)}, u32[]{:S(2)}) copy-start(f32[5,200]{1,0:T(8,128)} %copy-done.36) | copy-start | bytes 12004
  821.9 256.2 %copy-start.39 = (pred[5,200]{1,0:T(8,128)(4,1)S(1)}, pred[5,200]{1,0:T(8,128)(4,1)}, u32[]{:S(2)}) copy-start(pred[5,200]{1,0:T(8,128)(4,1)} %copy-done.38) | copy-start | bytes 3004
  821.9 256.2 %copy-start.41 = (f32[768]{0:T(1024)S(1)}, f32[768]{0:T(1024)}, u32[]{:S(2)}) copy-start(f32[768]{0:T(1024)} %param.29) | copy-start | bytes 9220
  832.6 248.4 %copy-start.45 = (f32[768]{0:T(1024)S(1)}, f32[768]{0:T(1024)}, u32[]{:S(2)}) copy-start(f32[768]{0:T(1024)} %param.35) | copy-start | bytes 9220
  1127.9 43.5 %copy-start.25 = (f32[192,768]{1,0:T(8,128)S(1)}, f32[192,768]{1,0:T(8,128)}, u32[]{:S(2)}) copy-start(f32[192,768]{1,0:T(8,128)} %get-tuple-element.655) | copy-start | bytes 1769476
  (40 other events, 148.3 us)
Sparse Core Ops, SparseCore 0:
  15.3 115.6 all-gather.4
  188.4 216.7 reduce-scatter.4
  564.6 111.1 all-gather.10
  776.3 106.7 reduce-scatter.6
  890.4 135.8 reduce-scatter.8
  1032.7 135.8 reduce-scatter.10
Sparse Core Ops, SparseCore 1:
  191.6 240.4 all-gather.6
  434.7 62.1 all-gather.8
  792.3 61.0 all-reduce.6
where the time goes:
time: 1190 us; the launch traced here: 1180 us
  waiting for transfers between devices  390 us (33%)
  other arithmetic  303 us (25%)
  matrix products  202 us (17%)
  local copies, waits for them, and re-layouts  151 us (13%)
  blocking collectives  117 us (10%)
  between operations  17 us (1%)
    scatter-add x1, other arithmetic, table_grad(): return start.at[rel_index.reshape(-1)].add(flat_grad)  216 us
    reduce_scatter x1, waiting for transfers between devices, on_device(): lax.psum_scatter(out_partial, 'head', scatter_dimension=0, tiled=True)  164 us
    all_gather x1, waiting for transfers between devices, on_device(): branch_rows = lax.all_gather(grad_branch, 'head', axis=0, tiled=True)  110 us
    gather x1, local copies, waits for them, and re-layouts, relative_bias(): picked = jnp.take(rel_table, rel_index.reshape(-1), axis=0)  74.2 us
    all_gather x1, waiting for transfers between devices, on_device(): lax.all_gather(down_weight, ('dp', 'head'), axis=0, tiled=True)  52.4 us
    unnamed x1, blocking collectives  48.2 us
    reduce_scatter x1, waiting for transfers between devices, on_device(): lax.psum_scatter(grad_down, ('dp', 'head'), scatter_dimension=0, tiled=True)  40.7 us
    psum x1, blocking collectives, on_device(): lax.psum((grad_mask_token, grad_attn_gain, grad_attn_shift, grad_out_bias...  40.5 us
  transfers between devices with their start and end apart: 9, of which 6 were waited for; matrix products, arithmetic and copies ran while one was open for 35% of the time, Pallas kernels for 0%

commit v1 on v0

v1 whole, which is shorter than its diff:
```python
from functools import partial

import jax
import jax.numpy as jnp
from jax import lax
from jax.experimental import pallas as pl
from jax.experimental.pallas import tpu as pltpu
from jax.sharding import PartitionSpec as P

HEAD_DIM = 64
SEQ = 200
VALID = 197
ROWS = 208
D = 768
HALF = 384
TABLE = 768
REACH = 384
CENTRE = 364
EPS = 1e-06
NEG = -1000000000.0
BOTH = ("dp", "head")
BF = jnp.bfloat16
F32 = jnp.float32
MIB = 1 << 20


def nn(a, b):
    return lax.dot_general(a, b, (((1,), (0,)), ((), ())), preferred_element_type=F32)


def nt(a, b):
    return lax.dot_general(a, b, (((1,), (1,)), ((), ())), preferred_element_type=F32)


def tn(a, b):
    return lax.dot_general(a, b, (((0,), (0,)), ((), ())), preferred_element_type=F32)


def norm_stats(rows):
    row_mean = jnp.mean(rows, axis=-1, keepdims=True)
    centered = rows - row_mean
    inv_std = lax.rsqrt(jnp.mean(centered * centered, axis=-1, keepdims=True) + EPS)
    return centered * inv_std, inv_std


def norm_back(grad_normed, normal, inv_std, gain):
    scaled = grad_normed * gain
    return inv_std * (
        scaled
        - jnp.mean(scaled, axis=-1, keepdims=True)
        - normal * jnp.mean(scaled * normal, axis=-1, keepdims=True)
    )


def swap_halves(core, value):
    low, high = value[:, :HALF], value[:, HALF:]
    first = core == 0
    return jnp.where(first, low, high), jnp.where(first, high, low)


def column_sum(value):
    return jnp.sum(value, axis=0, keepdims=True)


def split_two(value):
    high = value.astype(BF)
    return high, (value - high.astype(F32)).astype(BF)


def call(kernel, name, grid, in_specs, out_specs, out_shape, scratch=(), prefetch=0, vmem=48, flops=0, moved=0, aliases=None):
    return pl.pallas_call(
        kernel,
        name=name,
        grid_spec=pltpu.PrefetchScalarGridSpec(
            num_scalar_prefetch=prefetch,
            grid=grid,
            in_specs=in_specs,
            out_specs=out_specs,
            scratch_shapes=list(scratch),
        ),
        out_shape=out_shape,
        input_output_aliases=aliases or {},
        compiler_params=pltpu.CompilerParams(vmem_limit_bytes=vmem * MIB),
        cost_estimate=pl.CostEstimate(flops=int(flops), bytes_accessed=int(moved), transcendentals=0),
    )


def whole(shape):
    count = len(shape)
    return pl.BlockSpec(shape, lambda *_: (0,) * count)


def rows_of(width):
    return pl.BlockSpec((ROWS, width), lambda i, *_: (i, 0))


def image_of(width):
    return pl.BlockSpec((1, SEQ, width), lambda i, *_: (i, 0, 0))


def like(shape, dtype):
    return jax.ShapeDtypeStruct(shape, dtype)


def start_kernel(place, images, masked, out_grad, token, gain, shift, ffn_scale, normed, grad_mlp, sums):
    step = pl.program_id(0)
    hidden = jnp.where(masked[0] > 0.0, token[...], images[0].astype(F32))
    normal, _ = norm_stats(hidden)
    rows = normal * gain[...] + shift[...]
    low, high = swap_halves(place[0], rows)
    normed[0:SEQ, 0:HALF] = low.astype(BF)
    normed[0:SEQ, HALF:D] = high.astype(BF)
    normed[SEQ:ROWS, :] = jnp.zeros((ROWS - SEQ, D), BF)
    scaled = (out_grad[0].astype(F32) * ffn_scale[...]).astype(BF)
    grad_mlp[0:SEQ, :] = scaled
    grad_mlp[SEQ:ROWS, :] = jnp.zeros((ROWS - SEQ, D), BF)

    @pl.when(step == 0)
    def _():
        sums[...] = jnp.zeros_like(sums)

    sums[0:1, :] += column_sum(scaled.astype(F32))


def start(place, images, masked, out_grad, token, gain, shift, ffn_scale):
    count = images.shape[0]
    return call(
        start_kernel,
        "start",
        (count,),
        [image_of(D), image_of(1), image_of(D)] + [whole((1, D))] * 4,
        [rows_of(D), rows_of(D), whole((8, D))],
        [like((count * ROWS, D), BF), like((count * ROWS, D), BF), like((8, D), F32)],
        prefetch=1,
        flops=count * SEQ * D * 30,
        moved=count * SEQ * D * 8,
    )(place, images, masked, out_grad, token, gain, shift, ffn_scale)


def bias_kernel(spots_down, spots_across, edge_rows, table_ref, table_turned, bias, picked):
    heads = table_ref.shape[0]
    down = spots_down[...]
    across = spots_across[...]
    ones_down = (down == lax.broadcasted_iota(jnp.int32, (ROWS, REACH), 1)).astype(BF)
    ones_across = (across == lax.broadcasted_iota(jnp.int32, (REACH, ROWS), 0)).astype(BF)
    reach = lax.broadcasted_iota(jnp.int32, (ROWS, TABLE), 1)
    turned_high, turned_low = split_two(table_turned[...])
    for edge in range(SEQ - VALID):
        hot = (edge_rows[:, edge : edge + 1] == reach).astype(BF)
        picked[edge] = nn(hot, turned_high) + nn(hot, turned_low)
    key = lax.broadcasted_iota(jnp.int32, (ROWS, ROWS), 0)
    query = lax.broadcasted_iota(jnp.int32, (ROWS, ROWS), 1)
    for head in range(heads):
        line = table_ref[head : head + 1, :]
        spread = []
        for chunk in range(REACH // 128):
            turned = pltpu.roll(jnp.broadcast_to(line, (8, TABLE)), (TABLE - CENTRE + chunk * 128) % TABLE, 1)
            turned = jnp.broadcast_to(turned[0:1], (128, TABLE))
            spread.append(pltpu.roll(turned, 0, 1, stride=1, stride_axis=0)[:, :REACH])
        spread = jnp.concatenate(spread, axis=0)
        high, low = split_two(spread)
        middle = nn(nn(ones_down, high).astype(BF), ones_across)
        middle += nn(nn(ones_down, low).astype(BF), ones_across)
        value = jnp.where(key == 0, line[:, 730:731], middle)
        value = jnp.where(query == 0, jnp.where(key == 0, line[:, 731:732], line[:, 729:730]), value)
        for edge in range(SEQ - VALID):
            value = jnp.where(query == VALID + edge, picked[edge][:, head : head + 1], value)
        bias[head] = jnp.where(key >= VALID, NEG, value)


def bias_of(spots_down, spots_across, edge_rows, table, table_turned):
    heads = table.shape[0]
    return call(
        bias_kernel,
        "bias",
        (1,),
        [
            whole(spots_down.shape),
            whole(spots_across.shape),
            whole(edge_rows.shape),
            whole(table.shape),
            whole(table_turned.shape),
        ],
        whole((heads, ROWS, ROWS)),
        like((heads, ROWS, ROWS), F32),
        scratch=[pltpu.VMEM((SEQ - VALID, ROWS, 128), F32)],
        flops=heads * 4 * ROWS * REACH * REACH,
        moved=heads * ROWS * ROWS * 4,
    )(spots_down, spots_across, edge_rows, table, table_turned)


def table_kernel(spots_down, spots_across, edge_rows, grad_a, grad_b, out):
    each = grad_a.shape[0]
    down = spots_down[...]
    across = spots_across[...]
    ones_turned = ((REACH - 1) - across == lax.broadcasted_iota(jnp.int32, (REACH, ROWS), 0)).astype(BF)
    ones_turned = jnp.where(across >= 0, ones_turned, jnp.zeros_like(ones_turned))
    ones_down = (down == lax.broadcasted_iota(jnp.int32, (ROWS, REACH), 1)).astype(BF)
    reach = lax.broadcasted_iota(jnp.int32, (ROWS, TABLE), 1)
    line = lax.broadcasted_iota(jnp.int32, (1, TABLE), 1)
    key = lax.broadcasted_iota(jnp.int32, (ROWS, 1), 0)
    for head in range(2 * each):
        grads = grad_a if head < each else grad_b
        grad = grads[head % each]
        high, low = split_two(grad)
        both = nn(nn(ones_turned, high).astype(BF), ones_down)
        both += nn(nn(ones_turned, low).astype(BF), ones_down)
        total = jnp.zeros((1, TABLE), F32)
        for chunk in range(REACH // 128):
            rows = both[chunk * 128 : chunk * 128 + 128]
            wide = jnp.concatenate([rows, jnp.zeros((128, TABLE - REACH), F32)], axis=1)
            added = column_sum(pltpu.roll(wide, 0, 1, stride=1, stride_axis=0))
            shift = (TABLE - (REACH - 1 - CENTRE) + chunk * 128) % TABLE
            total += pltpu.roll(jnp.broadcast_to(added, (8, TABLE)), shift, 1)[0:1]
        first = grad[:, 0:1]
        total += jnp.where(line == 729, column_sum(jnp.where(key > 0, first, 0.0)), 0.0)
        total += jnp.where(line == 731, grad[0:1, 0:1], 0.0)
        top = lax.broadcasted_iota(jnp.int32, (1, ROWS), 1)
        row = jnp.where((top > 0) & (top < VALID), grad[0:1, :], 0.0)
        total += jnp.where(line == 730, jnp.sum(row, axis=1, keepdims=True), 0.0)
        for edge in range(SEQ - VALID):
            spot = edge_rows[:, edge : edge + 1] == reach
            total += column_sum(jnp.where(spot, grad[:, VALID + edge : VALID + edge + 1], 0.0))
        out[head : head + 1, :] = total


def table_of(spots_down, spots_across, edge_rows, grad_a, grad_b):
    heads = grad_a.shape[0] * 2
    return call(
        table_kernel,
        "table",
        (1,),
        [
            whole(spots_down.shape),
            whole(spots_across.shape),
            whole(edge_rows.shape),
            whole(grad_a.shape),
            whole(grad_b.shape),
        ],
        whole((heads, TABLE)),
        like((heads, TABLE), F32),
        flops=heads * 4 * ROWS * REACH * REACH,
        moved=heads * ROWS * ROWS * 4,
    )(spots_down, spots_across, edge_rows, grad_a, grad_b)


def project_kernel(mine, other, normed, bias, queries, keys, values, weights):
    planes, groups, blocks, part, _ = mine.shape
    heads = blocks // 4
    for plane in range(planes):
        for group in range(groups):
            for block in range(blocks):
                kind, head = divmod(block, heads)
                at = (group * heads + head) * HEAD_DIM + plane * part
                weights[kind, at : at + part, 0:HALF] = mine[plane, group, block]
                weights[kind, at : at + part, HALF:D] = other[plane, group, block]
    scale = HEAD_DIM ** (-0.5)
    queries[...] = ((nt(normed[...], weights[0]) + bias[0:1, :]) * scale).astype(BF)
    keys[...] = nt(normed[...], weights[1]).astype(BF)
    values[...] = (nt(normed[...], weights[2]) + bias[1:2, :]).astype(BF)


def project(mine, other, normed, bias):
    total = normed.shape[0]
    return call(
        project_kernel,
        "project",
        (1,),
        [whole(mine.shape), whole(other.shape), whole(normed.shape), whole(bias.shape)],
        [whole((total, HALF))] * 3 + [whole((4, HALF, D))],
        [like((total, HALF), BF)] * 3 + [like((4, HALF, D), BF)],
        flops=2 * total * D * HALF * 3,
        moved=8 * MIB,
    )(mine, other, normed, bias)


def attend_kernel(queries, keys, values, bias, attended, probs):
    lane = lax.broadcasted_iota(jnp.int32, (ROWS, 128), 1)
    for pair in range(HALF // 128):
        cols = slice(pair * 128, pair * 128 + 128)
        query_pair, key_pair = queries[:, cols], keys[:, cols]
        turned = values[:, cols].T
        parts = []
        for side in range(2):
            head = pair * 2 + side
            own = (lane >= 64) if side else (lane < 64)
            scores = nt(key_pair, jnp.where(own, query_pair, jnp.zeros_like(query_pair))) + bias[head]
            top = jnp.max(scores, axis=0, keepdims=True)
            expo = jnp.exp(scores - top)
            soft = (expo * (1.0 / jnp.sum(expo, axis=0, keepdims=True))).astype(BF)
            probs[0, head] = soft
            parts.append(nn(turned[side * 64 : side * 64 + 64, :], soft))
        attended[:, cols] = jnp.concatenate(parts, axis=0).T.astype(BF)


def attend(queries, keys, values, bias):
    total = queries.shape[0]
    count, heads = total // ROWS, bias.shape[0]
    return call(
        attend_kernel,
        "attend",
        (count,),
        [rows_of(HALF)] * 3 + [whole(bias.shape)],
        [rows_of(HALF), pl.BlockSpec((1, heads, ROWS, ROWS), lambda i: (i, 0, 0, 0))],
        [like((total, HALF), BF), like((count, heads, ROWS, ROWS), BF)],
        flops=4 * count * heads * ROWS * ROWS * 256,
        moved=10 * MIB,
    )(queries, keys, values, bias)


def attend_back_kernel(queries, keys, values, grad_att, probs, grad_q, grad_k, grad_v, grad_bias):
    step = pl.program_id(0)
    lane = lax.broadcasted_iota(jnp.int32, (ROWS, 128), 1)
    scale = HEAD_DIM ** (-0.5)

    @pl.when(step == 0)
    def _():
        grad_bias[...] = jnp.zeros_like(grad_bias)

    for pair in range(HALF // 128):
        cols = slice(pair * 128, pair * 128 + 128)
        query_pair, value_pair, grad_pair = queries[:, cols], values[:, cols], grad_att[:, cols]
        turned = keys[:, cols].T
        parts_q, parts_k, parts_v = [], [], []
        for side in range(2):
            head = pair * 2 + side
            own = (lane >= 64) if side else (lane < 64)
            soft = probs[0, head]
            wide = soft.astype(F32)
            grad_probs = nt(value_pair, jnp.where(own, grad_pair, jnp.zeros_like(grad_pair)))
            centre = jnp.sum(wide * grad_probs, axis=0, keepdims=True)
            grad_scores = (wide * (grad_probs - centre)).astype(BF)
            grad_bias[head] += grad_scores.astype(F32)
            parts_v.append(nn(soft, grad_pair))
            parts_k.append(nn(grad_scores, query_pair))
            parts_q.append(nn(turned[side * 64 : side * 64 + 64, :], grad_scores))
        grad_v[:, cols] = jnp.where(lane < 64, parts_v[0], parts_v[1]).astype(BF)
        grad_k[:, cols] = jnp.where(lane < 64, parts_k[0], parts_k[1]).astype(BF)
        grad_q[:, cols] = (jnp.concatenate(parts_q, axis=0).T * scale).astype(BF)


def attend_back(queries, keys, values, grad_att, probs):
    total = queries.shape[0]
    count, heads = probs.shape[:2]
    return call(
        attend_back_kernel,
        "attend_back",
        (count,),
        [rows_of(HALF)] * 4 + [pl.BlockSpec((1, heads, ROWS, ROWS), lambda i: (i, 0, 0, 0))],
        [rows_of(HALF)] * 3 + [whole((heads, ROWS, ROWS))],
        [like((total, HALF), BF)] * 3 + [like((heads, ROWS, ROWS), F32)],
        flops=10 * count * heads * ROWS * ROWS * 256,
        moved=10 * MIB,
    )(queries, keys, values, grad_att, probs)


def branch_kernel(
    place, att_a, att_b, out_a, out_b, images, masked, token, out_bias, attn_scale, gain, shift, branch, normed
):
    mixed = nn(att_a[...], out_a[0]) + nn(att_b[...], out_b[0])
    low, high = swap_halves(place[0], mixed)
    rows = jnp.concatenate([low, high], axis=1) + out_bias[...]
    branch[...] = rows
    hidden = jnp.where(masked[0] > 0.0, token[...], images[0].astype(F32))
    middle = hidden + attn_scale[...] * rows[0:SEQ]
    normal, _ = norm_stats(middle)
    normed[0:SEQ, :] = (normal * gain[...] + shift[...]).astype(BF)
    normed[SEQ:ROWS, :] = jnp.zeros((ROWS - SEQ, D), BF)


def out_weight_spec():
    return pl.BlockSpec((1, HALF, D), lambda i, *_: (3, 0, 0))


def branch_of(place, att_a, att_b, w_a, w_b, images, masked, vectors):
    count = images.shape[0]
    return call(
        branch_kernel,
        "branch",
        (count,),
        [rows_of(HALF), rows_of(HALF), out_weight_spec(), out_weight_spec(), image_of(D), image_of(1)]
        + [whole((1, D))] * len(vectors),
        [rows_of(D), rows_of(D)],
        [like((count * ROWS, D), F32), like((count * ROWS, D), BF)],
        prefetch=1,
        flops=2 * count * ROWS * D * D,
        moved=10 * MIB,
    )(place, att_a, att_b, w_a, w_b, images, masked, *vectors)


def gelu_both(value):
    cdf = 0.5 * (1.0 + lax.erf(value * (0.5**0.5)))
    pdf = jnp.exp(value * value * -0.5) * 0.3989422804014327
    return value * cdf, cdf + value * pdf


def feed_kernel(first, up_m, down_m, up_o, down_o, bias, normed, grad_mlp, *rest):
    if first:
        mlp, grad_normed, out_m, out_o, bias_grad, up, down, act, pre = rest
    else:
        _, _, mlp, grad_normed, out_m, out_o, bias_grad, up, down, act, pre = rest
    step = pl.program_id(0)
    half_steps = pl.num_programs(0) // 2
    slots, part = up_m.shape[0], up_m.shape[1]
    units = slots * part
    mine = step < half_steps

    def pick(up_ref, down_ref):
        for slot in range(slots):
            up[slot * part : slot * part + part, :] = up_ref[slot]
            down[slot * part : slot * part + part, :] = down_ref[slot]

    @pl.when(mine)
    def _():
        pick(up_m, down_m)

    @pl.when(jnp.logical_not(mine))
    def _():
        pick(up_o, down_o)

    if first:

        @pl.when(step == 0)
        def _():
            mlp[...] = jnp.zeros_like(mlp)
            grad_normed[...] = jnp.zeros_like(grad_normed)
    else:

        @pl.when(step == 0)
        def _():
            mlp[...] = rest[0][...]
            grad_normed[...] = rest[1][...]

    tiles = normed.shape[0] // ROWS

    def tile(index, total):
        at = pl.ds(pl.multiple_of(index * ROWS, ROWS), ROWS)
        value = nt(normed[at, :], up[...]) + bias[0]
        active, slope = gelu_both(value)
        act[at, :] = active.astype(BF)
        grad = (nt(grad_mlp[at, :], down[...]) * slope).astype(BF)
        pre[at, :] = grad
        return total + column_sum(grad.astype(F32))

    bias_grad[0] = lax.fori_loop(0, tiles, tile, jnp.zeros((1, units), F32))
    mlp[...] += nn(act[...], down[...])
    grad_normed[...] += nn(pre[...], up[...])
    grad_up = tn(pre[...], normed[...]).astype(BF)
    grad_down = tn(act[...], grad_mlp[...]).astype(BF)

    def put(ref):
        for slot in range(slots):
            ref[slot, 0:part, :] = grad_up[slot * part : slot * part + part, :]
            ref[slot, part : 2 * part, :] = grad_down[slot * part : slot * part + part, :]

    @pl.when(mine)
    def _():
        put(out_m)

    @pl.when(jnp.logical_not(mine))
    def _():
        put(out_o)


def feed(mine, other, bias, normed, grad_mlp, carried):
    total = normed.shape[0]
    slots, twice, _ = mine.shape
    part = twice // 2
    steps = bias.shape[0]
    take = 2 * slots // steps
    last = steps // 2 - 1
    first = carried is None

    def at_mine(place):
        return lambda i: (jnp.minimum(i, last), place, 0)

    def at_other(place):
        return lambda i: (jnp.maximum(i - last - 1, 0), place, 0)

    block = (take, part, D)
    wide = (take, twice, D)
    units = take * part
    in_specs = [
        pl.BlockSpec(block, at_mine(0)),
        pl.BlockSpec(block, at_mine(1)),
        pl.BlockSpec(block, at_other(0)),
        pl.BlockSpec(block, at_other(1)),
        pl.BlockSpec((1, 1, units), lambda i: (i, 0, 0)),
        whole((total, D)),
        whole((total, D)),
    ]
    operands = [mine, mine, other, other, bias, normed, grad_mlp]
    aliases = {}
    if not first:
        in_specs += [whole((total, D))] * 2
        operands += list(carried)
        aliases = {7: 0, 8: 1}
    return call(
        partial(feed_kernel, first),
        "feed",
        (steps,),
        in_specs,
        [
            whole((total, D)),
            whole((total, D)),
            pl.BlockSpec(wide, at_mine(0)),
            pl.BlockSpec(wide, at_other(0)),
            pl.BlockSpec((1, 1, units), lambda i: (i, 0, 0)),
        ],
        [
            like((total, D), F32),
            like((total, D), F32),
            like(mine.shape, BF),
            like(other.shape, BF),
            like(bias.shape, F32),
        ],
        scratch=[
            pltpu.VMEM((units, D), BF),
            pltpu.VMEM((units, D), BF),
            pltpu.VMEM((total, units), BF),
            pltpu.VMEM((total, units), BF),
        ],
        vmem=56,
        flops=12 * total * D * slots * part * 2,
        moved=20 * MIB,
        aliases=aliases,
    )(*operands)


def middle_kernel(
    place,
    mlp_ref,
    grad_normed,
    branch,
    images,
    masked,
    out_grad,
    out_a,
    out_b,
    token,
    attn_scale,
    gain,
    ffn_scale,
    down_bias,
    output,
    grad_middle,
    grad_branch,
    grad_a,
    grad_b,
    sums,
):
    step = pl.program_id(0)

    @pl.when(step == 0)
    def _():
        sums[...] = jnp.zeros_like(sums)

    hidden = jnp.where(masked[0] > 0.0, token[...], images[0].astype(F32))
    side = branch[0:SEQ, :]
    middle = hidden + attn_scale[...] * side
    mlp = mlp_ref[0:SEQ, :] + down_bias[...]
    output[0] = (middle + ffn_scale[...] * mlp).astype(BF)
    grad_out = out_grad[0].astype(F32)
    sums[0:1, :] += column_sum(grad_out * mlp)
    normal, inv_std = norm_stats(middle)
    grad_two = grad_normed[0:SEQ, :]
    sums[1:2, :] += column_sum(grad_two * normal)
    sums[2:3, :] += column_sum(grad_two)
    grad = grad_out + norm_back(grad_two, normal, inv_std, gain[...])
    grad_middle[0:SEQ, :] = grad
    grad_middle[SEQ:ROWS, :] = jnp.zeros((ROWS - SEQ, D), F32)
    sums[3:4, :] += column_sum(grad * side)
    low_branch = (grad * attn_scale[...]).astype(BF)
    sums[4:5, :] += column_sum(low_branch.astype(F32))
    low, high = swap_halves(place[0], low_branch)
    grad_branch[0:SEQ, 0:HALF] = low
    grad_branch[0:SEQ, HALF:D] = high
    grad_branch[SEQ:ROWS, :] = jnp.zeros((ROWS - SEQ, D), BF)
    grad_a[...] = nt(grad_branch[...], out_a[0]).astype(BF)
    grad_b[...] = nt(grad_branch[...], out_b[0]).astype(BF)


def middle_of(place, mlp, grad_normed, branch, images, masked, out_grad, w_a, w_b, vectors):
    count = images.shape[0]
    total = count * ROWS
    return call(
        middle_kernel,
        "middle",
        (count,),
        [rows_of(D)] * 3
        + [image_of(D), image_of(1), image_of(D), out_weight_spec(), out_weight_spec()]
        + [whole((1, D))] * len(vectors),
        [image_of(D), rows_of(D), rows_of(D), rows_of(HALF), rows_of(HALF), whole((8, D))],
        [
            like((count, SEQ, D), BF),
            like((total, D), F32),
            like((total, D), BF),
            like((total, HALF), BF),
            like((total, HALF), BF),
            like((8, D), F32),
        ],
        prefetch=1,
        flops=2 * total * D * D,
        moved=20 * MIB,
    )(place, mlp, grad_normed, branch, images, masked, out_grad, w_a, w_b, *vectors)


def weight_kernel(grad_q, grad_k, grad_v, attended, normed, grad_branch, mine, other, sums):
    planes, groups, blocks, part, _ = mine.shape
    heads = blocks // 4
    for kind, (left, right) in enumerate(
        ((grad_q, normed), (grad_k, normed), (grad_v, normed), (attended, grad_branch))
    ):
        grad = tn(left[...], right[...]).astype(BF)
        for plane in range(planes):
            for group in range(groups):
                for head in range(heads):
                    at = (group * heads + head) * HEAD_DIM + plane * part
                    mine[plane, group, kind * heads + head] = grad[at : at + part, 0:HALF]
                    other[plane, group, kind * heads + head] = grad[at : at + part, HALF:D]
    sums[...] = jnp.zeros_like(sums)
    sums[0:1, :] = column_sum(grad_q[...].astype(F32))
    sums[1:2, :] = column_sum(grad_v[...].astype(F32))


def weights_of(grads, attended, normed, grad_branch, shape):
    total = normed.shape[0]
    return call(
        weight_kernel,
        "weights",
        (1,),
        [whole((total, HALF))] * 4 + [whole((total, D))] * 2,
        [whole(shape), whole(shape), whole((8, HALF))],
        [like(shape, BF), like(shape, BF), like((8, HALF), F32)],
        flops=2 * total * D * HALF * 4,
        moved=10 * MIB,
    )(*grads, attended, normed, grad_branch)


def end_kernel(
    place, qa, ka, va, qb, kb, vb, w_a, w_b, grad_middle, images, masked, token, gain, images_grad, sums
):
    step = pl.program_id(0)

    @pl.when(step == 0)
    def _():
        sums[...] = jnp.zeros_like(sums)

    total = nn(qa[...], w_a[0]) + nn(ka[...], w_a[1]) + nn(va[...], w_a[2])
    total += nn(qb[...], w_b[0]) + nn(kb[...], w_b[1]) + nn(vb[...], w_b[2])
    low, high = swap_halves(place[0], total)
    grad_one = jnp.concatenate([low, high], axis=1)[0:SEQ]
    is_masked = masked[0] > 0.0
    hidden = jnp.where(is_masked, token[...], images[0].astype(F32))
    normal, inv_std = norm_stats(hidden)
    sums[0:1, :] += column_sum(grad_one * normal)
    sums[1:2, :] += column_sum(grad_one)
    grad = grad_middle[0:SEQ, :] + norm_back(grad_one, normal, inv_std, gain[...])
    images_grad[0] = jnp.where(is_masked, 0.0, grad).astype(BF)
    sums[2:3, :] += column_sum(jnp.where(is_masked, grad, 0.0))


def end_of(place, grads_a, grads_b, w_a, w_b, grad_middle, images, masked, vectors):
    count = images.shape[0]
    return call(
        end_kernel,
        "end",
        (count,),
        [rows_of(HALF)] * 6
        + [pl.BlockSpec((3, HALF, D), lambda i, *_: (0, 0, 0))] * 2
        + [rows_of(D), image_of(D), image_of(1)]
        + [whole((1, D))] * len(vectors),
        [image_of(D), whole((8, D))],
        [like((count, SEQ, D), BF), like((8, D), F32)],
        prefetch=1,
        flops=2 * count * ROWS * D * D * 3,
        moved=20 * MIB,
    )(place, *grads_a, *grads_b, w_a, w_b, grad_middle, images, masked, *vectors)


def order_kernel(place, gathered, qkv_grad, out_grad, wide):
    core, plane_here = place[0], place[1]
    _, planes, blocks, part, _ = gathered.shape
    heads = blocks // 4
    for plane in range(planes):
        slot = jnp.bitwise_xor(plane_here, plane)
        for block in range(blocks):
            at = block * HEAD_DIM + plane * part
            for half in range(2):
                from_core = jnp.bitwise_xor(core, half)
                wide[at : at + part, half * HALF : half * HALF + HALF] = gathered[
                    from_core, slot, block
                ].astype(F32)
    size = heads * HEAD_DIM
    for kind in range(3):
        qkv_grad[kind] = wide[kind * size : kind * size + size, :].T
    out_grad[...] = wide[3 * size : 4 * size, :]


def order(place, gathered):
    _, planes, blocks, part, _ = gathered.shape
    size = blocks // 4 * HEAD_DIM
    return call(
        order_kernel,
        "order",
        (1,),
        [whole(gathered.shape)],
        [whole((3, D, size)), whole((size, D))],
        [like((3, D, size), F32), like((size, D), F32)],
        scratch=[pltpu.VMEM((4 * size, D), F32)],
        prefetch=1,
        moved=5 * MIB,
    )(place, gathered)


class Butterfly:
    def __init__(self, mesh):
        self.dp, self.head = mesh.shape["dp"], mesh.shape["head"]
        self.far, self.near = 2, 1
        self.core, self.x, self.y = (self.head << bit for bit in range(3))

    def swap(self, value, mask):
        size = self.dp * self.head
        return lax.ppermute(value, BOTH, [(i, i ^ mask) for i in range(size)])

    def grow(self, value, mask):
        return jnp.stack([value, self.swap(value, mask)])

    def fold(self, value, mask):
        return add_low(value[0], self.swap(value[1], mask))


def add_low(own, come):
    return (own.astype(F32) + come.astype(F32)).astype(own.dtype)


def on_device(
    mesh,
    images,
    mask_ids,
    rel_index,
    out_grad,
    mask_token,
    attn_gain,
    attn_shift,
    qkv_weight,
    qv_bias,
    rel_table,
    out_weight,
    out_bias,
    attn_scale,
    ffn_gain,
    ffn_shift,
    up_weight,
    up_bias,
    down_weight,
    down_bias,
    ffn_scale,
):
    count = images.shape[0]
    heads = rel_table.shape[1]
    blocks = 4 * heads
    table_rows = rel_table.shape[0]
    own_units = up_weight.shape[1]
    positions = jnp.arange(SEQ, dtype=jnp.int32)
    masked = jnp.any(mask_ids[:, :, None] == positions, axis=1).astype(F32)[:, :, None]
    net = Butterfly(mesh)
    butterfly = net.dp == 8 and net.head == 4

    def line(vector):
        return vector.reshape(1, -1)

    stacked = jnp.concatenate([jnp.swapaxes(qkv_weight, 1, 2), out_weight[None]], axis=0)
    stacked = stacked.reshape(blocks, HEAD_DIM, D)
    small = jnp.zeros((8, D), F32)
    small = small.at[0:heads, :table_rows].set(rel_table.T)
    small = small.at[heads : heads + 2, : heads * HEAD_DIM].set(qv_bias)
    small = small.at[heads + 2, :own_units].set(up_bias.astype(F32))
    shares = jnp.stack([up_weight.T, down_weight])

    if butterfly:
        dp_here = lax.axis_index("dp")
        core = dp_here % 2
        plane = (dp_here // 2) % 2 * 2 + dp_here // 4
        place = jnp.stack([core, plane]).astype(jnp.int32)
        part = HEAD_DIM // 4
        own = lax.dynamic_slice(stacked, (0, plane * part, core * HALF), (blocks, part, HALF))
        attn = net.grow(net.grow(own, net.far), net.near)
        small_all = net.grow(net.grow(small, net.far), net.near)
        att_in_a = net.grow(net.grow(attn[0], net.y), net.x)
        att_in_b = net.grow(net.grow(attn[1], net.x), net.y)

        def planes(value):
            return value.reshape((4,) + value.shape[2:])

        def turn(value):
            value = jnp.where(dp_here // 2 % 2 == 1, value[:, :, :, ::-1], value)
            return jnp.where(dp_here // 4 == 1, value[:, :, :, :, ::-1], value)

        def by_slot(value):
            value = turn(value.reshape(2, 2, HALF // HEAD_DIM, 2, 2, part))
            return jnp.stack([value[0], value[1].swapaxes(2, 3)]).reshape(2, 2, HALF)

        def by_place(value):
            value = value.reshape(2, 2, HALF // HEAD_DIM, 2, 2, part)
            return turn(jnp.stack([value[0], value[1].swapaxes(2, 3)])).reshape(2, 2, HALF)

        att_in_a, att_in_b = planes(att_in_a), planes(att_in_b)
        attn_pieces = [(v, net.swap(v, net.core)) for v in (att_in_a, att_in_b)]

        half_units = own_units // 2
        ffn = shares.reshape(2, 2, half_units, D).transpose(1, 0, 2, 3).reshape(2, 2 * half_units, D)
        ffn = net.grow(net.grow(ffn, net.far), net.near).reshape(4, 2, 2 * half_units, D)
        ffn_in_a = net.grow(net.grow(ffn[:, 0], net.y), net.x).reshape(16, 2 * half_units, D)
        ffn_in_b = net.grow(net.grow(ffn[:, 1], net.x), net.y).reshape(16, 2 * half_units, D)
        ffn_pieces = [(v, net.swap(v, net.core)) for v in (ffn_in_a, ffn_in_b)]
        unit_bias = small_all[:, :, heads + 2, :own_units].reshape(4, own_units)
        unit_bias = net.grow(net.grow(net.grow(unit_bias, net.y), net.x), net.core)
        bias_a = unit_bias[..., :half_units].reshape(4, 1, -1)
        bias_b = unit_bias[..., half_units:].transpose(0, 2, 1, 3, 4).reshape(4, 1, -1)
        unit_biases = [bias_a, bias_b]
        small_all = small_all.reshape(4, 8, D)
    else:
        place = jnp.zeros((2,), jnp.int32)
        part = HEAD_DIM // 4
        by_slot = by_place = lambda value: value
        gathered = lax.all_gather(stacked, "head", axis=0, tiled=False)
        gathered = gathered.reshape(2, 2, blocks, 4, part, 2, HALF).transpose(0, 5, 3, 1, 2, 4, 6)
        attn_pieces = [(gathered[i, 0], gathered[i, 1]) for i in range(2)]
        ffn = lax.all_gather(shares, BOTH, axis=1, tiled=True)
        units_all = ffn.shape[1]
        half_units = units_all // 64
        ffn = ffn.reshape(2, 2, 2, 16, half_units, D).transpose(1, 2, 3, 0, 4, 5)
        ffn = ffn.reshape(2, 2, 16, 2 * half_units, D)
        ffn_pieces = [(ffn[i, 0], ffn[i, 1]) for i in range(2)]
        small_all = lax.all_gather(small, "head", axis=0, tiled=False)
        unit_bias = lax.all_gather(up_bias.astype(F32), BOTH, axis=0, tiled=True)
        unit_bias = unit_bias.reshape(2, 4, 1, -1)
        unit_biases = [unit_bias[0], unit_bias[1]]

    groups = small_all.shape[0]
    normed_one, grad_mlp, sums_start = start(
        place, images, masked, out_grad, line(mask_token), line(attn_gain), line(attn_shift), line(ffn_scale)
    )

    column = rel_index[:, 1]
    patch = (positions >= 1) & (positions < VALID)
    corner = jnp.min(jnp.where(patch, column, TABLE))
    spots = jnp.where(patch, column - corner, -1)
    spots = jnp.pad(spots, (0, ROWS - SEQ), constant_values=-1)
    spots_down, spots_across = spots[:, None], spots[None, :]
    edge_rows = jnp.pad(rel_index[VALID:, :].T, ((0, ROWS - SEQ), (0, 8 - (SEQ - VALID))))
    table = small_all[:, :heads].reshape(groups * heads, TABLE)
    table_turned = jnp.pad(table.T, ((0, 0), (0, 128 - groups * heads)))
    bias = bias_of(spots_down, spots_across, edge_rows, table, table_turned)
    each = groups * heads // 2
    qv_all = small_all[:, heads : heads + 2, : heads * HEAD_DIM].reshape(2, groups // 2, 2, heads * HEAD_DIM)
    qv_all = by_slot(qv_all.transpose(0, 2, 1, 3).reshape(2, 2, HALF))

    streams = []
    for half in range(2):
        mine, other = attn_pieces[half]
        queries, keys, values, weights = project(mine, other, normed_one, qv_all[half])
        attended, probs = attend(queries, keys, values, bias[half * each : half * each + each])
        streams.append((queries, keys, values, weights, attended, probs))
    w_a, w_b = streams[0][3], streams[1][3]
    branch, normed_two = branch_of(
        place,
        streams[0][4],
        streams[1][4],
        w_a,
        w_b,
        images,
        masked,
        [line(v) for v in (mask_token, out_bias, attn_scale, ffn_gain, ffn_shift)],
    )

    carried = None
    ffn_grads, unit_grads = [], []
    for half in range(2):
        mine, other = ffn_pieces[half]
        mlp, grad_two, grad_m, grad_o, unit_grad = feed(
            mine, other, unit_biases[half], normed_two, grad_mlp, carried
        )
        carried = (mlp, grad_two)
        ffn_grads.append((grad_m, grad_o))
        unit_grads.append(unit_grad)
    output, grad_middle, grad_branch, grad_att_a, grad_att_b, sums_middle = middle_of(
        place,
        carried[0],
        carried[1],
        branch,
        images,
        masked,
        out_grad,
        w_a,
        w_b,
        [line(v) for v in (mask_token, attn_scale, ffn_gain, ffn_scale, down_bias)],
    )
    back, grad_biases = [None, None], [None, None]
    attn_grads, qv_sums = [None, None], [None, None]
    for half in (1, 0):
        queries, keys, values, _, attended, probs = streams[half]
        grad_att = grad_att_a if half == 0 else grad_att_b
        *grads, grad_biases[half] = attend_back(queries, keys, values, grad_att, probs)
        back[half] = grads
        grad_m, grad_o, qv_sums[half] = weights_of(
            grads, attended, normed_one, grad_branch, attn_pieces[half][0].shape
        )
        attn_grads[half] = (grad_m, grad_o)
    images_grad, sums_end = end_of(
        place, back[0], back[1], w_a, w_b, grad_middle, images, masked, [line(mask_token), line(attn_gain)]
    )
    grad_table = table_of(spots_down, spots_across, edge_rows, grad_biases[0], grad_biases[1])

    vectors = jnp.concatenate([sums_start[0:1], sums_middle[0:5], sums_end[0:3]], axis=0)
    qv_grad = by_place(jnp.stack([qv_sums[0][0:2], qv_sums[1][0:2]]))
    qv_grad = qv_grad.reshape(2, 2, groups // 2, heads * HEAD_DIM).transpose(0, 2, 1, 3)
    slots = jnp.concatenate(
        [
            grad_table.reshape(groups, heads, TABLE),
            jnp.pad(qv_grad.reshape(groups, 2, -1), ((0, 0), (0, 0), (0, D - heads * HEAD_DIM))),
        ],
        axis=1,
    )
    extra = slots.shape[1]

    if butterfly:
        sum_a = add_low(ffn_grads[0][0], net.swap(ffn_grads[0][1], net.core))
        sum_b = add_low(ffn_grads[1][0], net.swap(ffn_grads[1][1], net.core))
        tall = 2 * half_units
        sum_a = net.fold(net.fold(sum_a.reshape(2, 2, 4, tall, D), net.x), net.y)
        sum_b = net.fold(net.fold(sum_b.reshape(2, 2, 4, tall, D), net.y), net.x)
        both = jnp.stack([sum_a, sum_b], axis=1).reshape(2, 2, 2, tall, D)
        both = net.fold(net.fold(both, net.near), net.far)
        both = both.reshape(2, 2, half_units, D).transpose(1, 0, 2, 3).reshape(2, own_units, D)
        own_ffn = both.astype(F32)

        sum_b = add_low(attn_grads[1][0], net.swap(attn_grads[1][1], net.core))
        sum_b = net.fold(net.fold(sum_b.reshape((2, 2) + sum_b.shape[1:]), net.y), net.x)
        come = net.swap(sum_b, net.near)
        sum_a = add_low(attn_grads[0][0], net.swap(attn_grads[0][1], net.core))
        sum_a = net.fold(net.fold(sum_a.reshape((2, 2) + sum_a.shape[1:]), net.x), net.y)
        own = net.fold(add_low(sum_a, come), net.far)
        own = net.grow(net.grow(net.grow(own, net.y), net.x), net.core)
        gathered = own.reshape((2, 4) + own.shape[3:])

        units_a = unit_grads[0].reshape(2, 2, 2, 4, half_units)
        units_b = unit_grads[1].reshape(2, 2, 2, 4, half_units).transpose(0, 2, 1, 3, 4)
        units = jnp.concatenate([units_a, units_b], axis=-1)
        units = units.transpose(3, 0, 1, 2, 4).reshape(4, 2, 2, 2, own_units)
        rows = vectors.shape[0] * D
        vectors, slots = vectors.reshape(-1), slots.reshape(groups, -1)
        for mask in (net.near, net.far):
            slots, slots_out = jnp.split(slots, 2)
            units, units_out = jnp.split(units, 2)
            sent = jnp.concatenate([vectors, slots_out.reshape(-1), units_out.reshape(-1)])
            come = net.swap(sent, mask)
            vectors = vectors + come[:rows]
            slots = slots + come[rows : rows + slots.size].reshape(slots.shape)
            units = units + come[rows + slots.size :].reshape(units.shape)
        vectors = jnp.concatenate([vectors, slots.reshape(-1)])
        units = units[0]
        for axis, mask in ((2, net.y), (1, net.x), (0, net.core)):
            units, units_out = jnp.split(units, 2, axis=axis)
            come = net.swap(jnp.concatenate([vectors, units_out.reshape(-1)]), mask)
            vectors = vectors + come[: vectors.size]
            units = units + come[vectors.size :].reshape(units.shape)
        slots = vectors[rows:].reshape(extra, D)
        vectors = vectors[:rows].reshape(-1, D)
        up_bias_grad = units.reshape(own_units)
    else:
        parts = jnp.stack([jnp.stack(attn_grads[i]) for i in range(2)]).astype(F32)
        parts = parts.transpose(0, 3, 4, 2, 5, 1, 6).reshape(groups, blocks, HEAD_DIM, D)
        own = lax.psum_scatter(parts, "head", scatter_dimension=0, tiled=True)
        own = lax.psum(own, "dp").reshape(blocks, 4, part, 2, HALF)
        gathered = own.transpose(3, 1, 0, 2, 4)
        both = jnp.stack([jnp.stack(ffn_grads[i]) for i in range(2)]).astype(F32)
        both = both.reshape(2, 2, 16, 2, half_units, D).transpose(3, 0, 1, 2, 4, 5)
        own_ffn = lax.psum_scatter(
            both.reshape(2, -1, D), BOTH, scatter_dimension=1, tiled=True
        )
        units = jnp.stack(unit_grads).reshape(-1)
        up_bias_grad = lax.psum_scatter(units, BOTH, scatter_dimension=0, tiled=True)
        vectors = lax.psum(vectors, BOTH)
        slots = lax.psum_scatter(slots, "head", scatter_dimension=0, tiled=True)[0]
        slots = lax.psum(slots, "dp")

    qkv_weight_grad, out_weight_grad = order(place, gathered)
    (
        down_bias_grad,
        ffn_scale_grad,
        ffn_gain_grad,
        ffn_shift_grad,
        attn_scale_grad,
        out_bias_grad,
        attn_gain_grad,
        attn_shift_grad,
        mask_token_grad,
    ) = vectors
    return (
        output,
        images_grad,
        mask_token_grad,
        attn_gain_grad,
        attn_shift_grad,
        qkv_weight_grad,
        slots[heads : heads + 2, : heads * HEAD_DIM],
        slots[:heads, :table_rows].T,
        out_weight_grad,
        out_bias_grad,
        attn_scale_grad,
        ffn_gain_grad,
        ffn_shift_grad,
        own_ffn[0].T,
        up_bias_grad,
        own_ffn[1],
        down_bias_grad,
        ffn_scale_grad,
    )


def solution(mesh):
    in_specs = (
        P(("dp", "head"), None, None),
        P(("dp", "head"), None),
        P(),
        P(("dp", "head"), None, None),
        P(),
        P(),
        P(),
        P(None, None, "head"),
        P(None, "head"),
        P(None, "head"),
        P("head", None),
        P(),
        P(),
        P(),
        P(),
        P(None, ("dp", "head")),
        P(("dp", "head")),
        P(("dp", "head"), None),
        P(),
        P(),
    )
    out_specs = (
        P(("dp", "head"), None, None),
        P(("dp", "head"), None, None),
        P(),
        P(),
        P(),
        P(None, None, "head"),
        P(None, "head"),
        P(None, "head"),
        P("head", None),
        P(),
        P(),
        P(),
        P(),
        P(None, ("dp", "head")),
        P(("dp", "head")),
        P(("dp", "head"), None),
        P(),
        P(),
    )
    return jax.shard_map(
        partial(on_device, mesh), mesh=mesh, in_specs=in_specs, out_specs=out_specs, check_vma=False
    )
```

time: 1190 us -> 448 us (0.38)
  other arithmetic: 303 us -> 39.8 us
  waiting for transfers between devices: 390 us -> 134 us
  matrix products: 202 us -> 0 us
  Pallas kernels: 0 us -> 180 us
  blocking collectives: 117 us -> 0 us
  local copies, waits for them, and re-layouts: 151 us -> 39.5 us
  starting transfers between devices: 0.37 us -> 47.9 us
  between operations: 17 us -> 2.21 us
    scatter-add x1 -> x0, other arithmetic: 216 us -> none  [table_grad(): return start.at[rel_index.reshape(-1)].add(flat_grad)]
    reduce_scatter x4 -> x0, waiting for transfers between devices: 204 us -> none  [the longest x1 164 us: on_device(): lax.psum_scatter(out_partial, 'head', scatter_dimension=0, tiled=True)]
    dot_general x47 -> x0, matrix products: 202 us -> none  [the longest x1 36 us: on_device(): jnp.einsum('rd,fd->rf', grad_mlp_flat, down_full, preferred_element_type=...]
    all_gather x4 -> x0, waiting for transfers between devices: 184 us -> none  [the longest x1 110 us: on_device(): branch_rows = lax.all_gather(grad_branch, 'head', axis=0, tiled=True)]
    pallas_call x0 -> x17, Pallas kernels: none -> 180 us  [the longest x2 66.4 us: feed(): call(partial(feed_kernel, first), 'feed', (steps,), in_specs, [whole((tot...]
    ppermute x0 -> x45, waiting for transfers between devices: none -> 134 us  [swap(): return lax.ppermute(value, BOTH, [(i, i ^ mask) for i in range(size)])]
    gather x1 -> x0, local copies, waits for them, and re-layouts: 74.2 us -> none  [relative_bias(): picked = jnp.take(rel_table, rel_index.reshape(-1), axis=0)]
    psum x2 -> x0, blocking collectives: 69.1 us -> none  [the longest x1 40.5 us: on_device(): lax.psum((grad_mask_token, grad_attn_gain, grad_attn_shift, grad_out_bias...]
  transfers between devices with their start and end apart: 9 -> 45, of which waited for: 6 -> 21; matrix products, arithmetic and copies ran while one was open for 35% -> 15% of each run, Pallas kernels for 0% -> 18%
where the time goes in v1:
time: 448 us; the launch traced here: 444 us
  Pallas kernels  180 us (40%)
  waiting for transfers between devices  134 us (30%)
  starting transfers between devices  47.9 us (11%)
  other arithmetic  39.8 us (9%)
  local copies, waits for them, and re-layouts  39.5 us (9%)
    ppermute x45, waiting for transfers between devices, swap(): return lax.ppermute(value, BOTH, [(i, i ^ mask) for i in range(size)])  134 us
    pallas_call x2, Pallas kernels, feed(): call(partial(feed_kernel, first), 'feed', (steps,), in_specs, [whole((tot...  66.4 us
    ppermute x45, starting transfers between devices, swap(): return lax.ppermute(value, BOTH, [(i, i ^ mask) for i in range(size)])  47.9 us
    another operation x20, other arithmetic, grow(): return jnp.stack([value, self.swap(value, mask)])  24.1 us
    pallas_call x2, Pallas kernels, attend_back(): call(attend_back_kernel, 'attend_back', (count,), [rows_of(HALF)] * 4 + [...  21.9 us
    pallas_call x2, Pallas kernels, attend(): call(attend_kernel, 'attend', (count,), [rows_of(HALF)] * 3 + [whole(bias...  18 us
    pallas_call x2, Pallas kernels, project(): call(project_kernel, 'project', (1,), [whole(mine.shape), whole(other.sha...  12.7 us
    pallas_call x1, Pallas kernels, end_of(): call(end_kernel, 'end', (count,), [rows_of(HALF)] * 6 + [pl.BlockSpec((3,...  12.3 us
  transfers between devices with their start and end apart: 45, of which 21 were waited for; matrix products, arithmetic and copies ran while one was open for 15% of the time, Pallas kernels for 18%

profile of v1, /device:TPU:0, one launch (start us, length us, event | category | flops | bytes accessed | tf_op | source)
XLA Modules:
  0.0 443.8 jit_solution(1627634397734636937)
XLA Ops:
  1.8 4.1 collective-permute-start
  8.2 11.1 %collective-permute-done = bf16[2,96,768]{2,1,0:T(8,128)(2,1)S(1)} collective-permute-done((bf16[2,96,768]{2,1,0:T(8,128)(2,1)S(1)}, bf16[2,96,768]{2,1,0:T(8,128)(2,1)S(1)}, u32[]{:S(2)}, u32[]{:S(2)}) %collective-permute-start) | collective-permute-done | bytes 294944 | tf_op jit(solution)/shard_map/ppermute | solution.py:724
  24.8 12.8 %collective-permute-done.1 = bf16[2,2,96,768]{3,2,1,0:T(8,128)(2,1)S(1)} collective-permute-done((bf16[2,2,96,768]{3,2,1,0:T(8,128)(2,1)S(1)}, bf16[2,2,96,768]{3,2,1,0:T(8,128)(2,1)S(1)}, u32[]{:S(2)}, u32[]{:S(2)}) %collective-permute-start.1) | collective-permute-done | bytes 589856 | tf_op jit(solution)/shard_map/ppermute | solution.py:724
  41.6 10.9 %collective-permute-done.18 = bf16[4,96,768]{2,1,0:T(8,128)(2,1)S(1)} collective-permute-done((bf16[4,96,768]{2,1,0:T(8,128)(2,1)S(1)}, bf16[4,96,768]{2,1,0:T(8,128)(2,1)S(1)}, u32[]{:S(2)}, u32[]{:S(2)}) %collective-permute-start.18) | collective-permute-done | bytes 589856 | tf_op jit(solution)/shard_map/ppermute | solution.py:724
  64.3 4.6 %start.1 = (bf16[1040,768]{1,0:T(8,128)(2,1)S(1)}, bf16[1040,768]{1,0:T(8,128)(2,1)}, f32[8,768]{1,0:T(8,128)S(1)}) custom-call(s32[2]{0:T(128)S(1)} %pad_add_fusion.place, bf16[5,200,768]{2,1,0:T(8,128)(2,1)S(1)} %copy-done, f32[5,200,1]{2,1,0:T(8,128)S(1)} %copy.76.masked, bf16[5,200,768]{2,1,0:T(8,128)(2,1)S(1)} %copy-done.1, ...), custom_call_target="tpu_custom_call" | custom-call | flops 23040000 | bytes 6144000 | tf_op jit(solution)/shard_map/start/pallas_call | solution.py:127
  81.1 5.7 %bias.1 = f32[12,208,208]{2,1,0:T(8,128)S(1)} custom-call(s32[208,1]{1,0:T(8,128)S(1)} %copy.80.spots_down, s32[1,208]{1,0:T(1,128)S(1)} %bitcast.197, s32[208,8]{1,0:T(8,128)S(1)} %pad.30.edge_rows, f32[12,768]{1,0:T(8,128)S(1)} %reshape.419.table_ref, f32[768,128]{1,0:T(8,128)S(1)} %pad.31.table_turned), custom_call_target="tpu_custom_call" | custom-call | flops 1472200704 | bytes 2076672 | tf_op jit(solution)/shard_map/bias/pallas_call | solution.py:173
  89.1 12.9 %collective-permute-done.15 = bf16[2,12,16,384]{3,2,1,0:T(8,128)(2,1)} collective-permute-done((bf16[2,12,16,384]{3,2,1,0:T(8,128)(2,1)}, bf16[2,12,16,384]{3,2,1,0:T(8,128)(2,1)}, u32[]{:S(2)}, u32[]{:S(2)}) %collective-permute-start.15) | collective-permute-done | bytes 294944 | tf_op jit(solution)/shard_map/ppermute | solution.py:724
  116.8 4.0 collective-permute-done.16
  128.2 9.7 %collective-permute-done.3 = bf16[2,4,96,768]{3,2,1,0:T(8,128)(2,1)} collective-permute-done((bf16[2,4,96,768]{3,2,1,0:T(8,128)(2,1)}, bf16[2,4,96,768]{3,2,1,0:T(8,128)(2,1)}, u32[]{:S(2)}, u32[]{:S(2)}) %collective-permute-start.3) | collective-permute-done | bytes 1179680 | tf_op jit(solution)/shard_map/ppermute | solution.py:724
  150.5 6.4 %project.2 = (bf16[1040,384]{1,0:T(8,128)(2,1)S(1)}, bf16[1040,384]{1,0:T(8,128)(2,1)S(1)}, bf16[1040,384]{1,0:T(8,128)(2,1)S(1)}, bf16[4,384,768]{2,1,0:T(8,128)(2,1)}) custom-call(bf16[4,2,12,16,384]{4,3,2,1,0:T(8,128)(2,1)} %bitcast.42.mine, bf16[4,2,12,16,384]{4,3,2,1,0:T(8,128)(2,1)} %collective-permute-done.13.other, bf16[1040,768]{1,0:T(8,128)(2,1)} %copy-done.16, ...), custom_call_target="tpu_custom_call" | custom-call | flops 1840250880 | bytes 8388608 | tf_op jit(solution)/shard_map/project/pallas_call | solution.py:265
  156.9 9.1 %attend.2 = (bf16[1040,384]{1,0:T(8,128)(2,1)S(1)}, bf16[5,6,208,208]{3,2,1,0:T(8,128)(2,1)}) custom-call(bf16[1040,384]{1,0:T(8,128)(2,1)S(1)} %get-tuple-element.106.queries, bf16[1040,384]{1,0:T(8,128)(2,1)S(1)} %get-tuple-element.107.keys, bf16[1040,384]{1,0:T(8,128)(2,1)S(1)} %get-tuple-element.108.values, f32[6,208,208]{2,1,0:T(8,128)S(1)} %copy-done.3), custom_call_target="tpu_custom_call" | custom-call | flops 1329070080 | bytes 10485760 | tf_op jit(solution)/shard_map/attend/pallas_call | solution.py:299
  166.1 6.3 %project.3 = (bf16[1040,384]{1,0:T(8,128)(2,1)S(1)}, bf16[1040,384]{1,0:T(8,128)(2,1)S(1)}, bf16[1040,384]{1,0:T(8,128)(2,1)S(1)}, bf16[4,384,768]{2,1,0:T(8,128)(2,1)}) custom-call(bf16[4,2,12,16,384]{4,3,2,1,0:T(8,128)(2,1)} %bitcast.55.mine, bf16[4,2,12,16,384]{4,3,2,1,0:T(8,128)(2,1)} %collective-permute-done.17.other, bf16[1040,768]{1,0:T(8,128)(2,1)} %copy-done.16, ...), custom_call_target="tpu_custom_call" | custom-call | flops 1840250880 | bytes 8388608 | tf_op jit(solution)/shard_map/project/pallas_call | solution.py:265
  172.4 8.9 %attend.3 = (bf16[1040,384]{1,0:T(8,128)(2,1)S(1)}, bf16[5,6,208,208]{3,2,1,0:T(8,128)(2,1)}) custom-call(bf16[1040,384]{1,0:T(8,128)(2,1)S(1)} %get-tuple-element.110.queries, bf16[1040,384]{1,0:T(8,128)(2,1)S(1)} %get-tuple-element.111.keys, bf16[1040,384]{1,0:T(8,128)(2,1)S(1)} %get-tuple-element.112.values, f32[6,208,208]{2,1,0:T(8,128)S(1)} %get-tuple-element.210.bias), custom_call_target="tpu_custom_call" | custom-call | flops 1329070080 | bytes 10485760 | tf_op jit(solution)/shard_map/attend/pallas_call | solution.py:299
  181.4 6.3 %branch.1 = (f32[1040,768]{1,0:T(8,128)}, bf16[1040,768]{1,0:T(8,128)(2,1)S(1)}) custom-call(s32[2]{0:T(128)S(1)} %copy-done.7, bf16[1040,384]{1,0:T(8,128)(2,1)S(1)} %get-tuple-element.109.att_a.attended, bf16[1040,384]{1,0:T(8,128)(2,1)S(1)} %get-tuple-element.113.att_b.attended, bf16[4,384,768]{2,1,0:T(8,128)(2,1)} %get-tuple-element.114.out_a.w_a, ...), custom_call_target="tpu_custom_call" | custom-call | flops 1226833920 | bytes 10485760 | tf_op jit(solution)/shard_map/branch/pallas_call | solution.py:377
  188.9 32.2 %feed.2 = (f32[1040,768]{1,0:T(8,128)}, f32[1040,768]{1,0:T(8,128)}, bf16[16,96,768]{2,1,0:T(8,128)(2,1)}, bf16[16,96,768]{2,1,0:T(8,128)(2,1)}, f32[4,1,384]{2,1,0:T(1,128)}) custom-call(bf16[16,96,768]{2,1,0:T(8,128)(2,1)} %bitcast.63.up_m.down_m, bf16[16,96,768]{2,1,0:T(8,128)(2,1)} %bitcast.63.up_m.down_m, ...), custom_call_target="tpu_custom_call" | custom-call | flops 14722007040 | bytes 20971520 | tf_op jit(solution)/shard_map/feed/pallas_call | solution.py:498
  221.1 34.2 %feed.3 = (f32[1040,768]{1,0:T(8,128)}, f32[1040,768]{1,0:T(8,128)}, bf16[16,96,768]{2,1,0:T(8,128)(2,1)}, bf16[16,96,768]{2,1,0:T(8,128)(2,1)}, f32[4,1,384]{2,1,0:T(1,128)}) custom-call(bf16[16,96,768]{2,1,0:T(8,128)(2,1)} %bitcast.17.up_m.down_m, bf16[16,96,768]{2,1,0:T(8,128)(2,1)} %bitcast.17.up_m.down_m, ...), custom_call_target="tpu_custom_call", output_to_operand_aliasing={{0}: (7, {}), {1}: (8, {})} | custom-call | flops 14722007040 | bytes 20971520 | tf_op jit(solution)/shard_map/feed/pallas_call | solution.py:498
  255.4 11.1 %middle.1 = (bf16[5,200,768]{2,1,0:T(8,128)(2,1)}, f32[1040,768]{1,0:T(8,128)}, bf16[1040,768]{1,0:T(8,128)(2,1)}, bf16[1040,384]{1,0:T(8,128)(2,1)S(1)}, bf16[1...) custom-call(s32[2]{0:T(128)S(1)} %copy-done.7, f32[1040,768]{1,0:T(8,128)} %get-tuple-element.120.mlp_ref, ...), custom_call_target="tpu_custom_call" | custom-call | flops 1226833920 | bytes 20971520 | tf_op jit(solution)/shard_map/middle/pallas_call | solution.py:586
  266.5 11.0 %attend_back.3 = (bf16[1040,384]{1,0:T(8,128)(2,1)S(1)}, bf16[1040,384]{1,0:T(8,128)(2,1)S(1)}, bf16[1040,384]{1,0:T(8,128)(2,1)S(1)}, f32[6,208,208]{2,1,0:T(8,128)}) custom-call(bf16[1040,384]{1,0:T(8,128)(2,1)S(1)} %copy-done.27, bf16[1040,384]{1,0:T(8,128)(2,1)S(1)} %copy-done.29, bf16[1040,384]{1,0:T(8,128)(2,1)S(1)} %copy-done.31, ...), custom_call_target="tpu_custom_call" | custom-call | flops 3322675200 | bytes 10485760 | tf_op jit(solution)/shard_map/attend_back/pallas_call | solution.py:345
  277.5 10.9 %attend_back.2 = (bf16[1040,384]{1,0:T(8,128)(2,1)S(1)}, bf16[1040,384]{1,0:T(8,128)(2,1)S(1)}, bf16[1040,384]{1,0:T(8,128)(2,1)S(1)}, f32[6,208,208]{2,1,0:T(8,128)}) custom-call(bf16[1040,384]{1,0:T(8,128)(2,1)S(1)} %copy-done.21, bf16[1040,384]{1,0:T(8,128)(2,1)S(1)} %copy-done.23, bf16[1040,384]{1,0:T(8,128)(2,1)S(1)} %copy-done.25, ...), custom_call_target="tpu_custom_call" | custom-call | flops 3322675200 | bytes 10485760 | tf_op jit(solution)/shard_map/attend_back/pallas_call | solution.py:345
  288.4 5.2 %weights.3 = (bf16[4,2,12,16,384]{4,3,2,1,0:T(8,128)(2,1)S(1)}, bf16[4,2,12,16,384]{4,3,2,1,0:T(8,128)(2,1)S(1)}, f32[8,384]{1,0:T(8,128)S(1)}) custom-call(bf16[1040,384]{1,0:T(8,128)(2,1)S(1)} %get-tuple-element.131.qb.grad_q, bf16[1040,384]{1,0:T(8,128)(2,1)S(1)} %get-tuple-element.132.kb.grad_k, bf16[1040,384]{1,0:T(8,128)(2,1)S(1)} %get-tuple-element.133.vb.grad_v, ...), custom_call_target="tpu_custom_call" | custom-call | flops 2453667840 | bytes 10485760 | tf_op jit(solution)/shard_map/weights/pallas_call | solution.py:628
  294.6 5.2 %weights.2 = (bf16[4,2,12,16,384]{4,3,2,1,0:T(8,128)(2,1)S(1)}, bf16[4,2,12,16,384]{4,3,2,1,0:T(8,128)(2,1)S(1)}, f32[8,384]{1,0:T(8,128)S(1)}) custom-call(bf16[1040,384]{1,0:T(8,128)(2,1)S(1)} %get-tuple-element.126.qa.grad_q, bf16[1040,384]{1,0:T(8,128)(2,1)S(1)} %get-tuple-element.127.ka.grad_k, bf16[1040,384]{1,0:T(8,128)(2,1)S(1)} %get-tuple-element.128.va.grad_v, ...), custom_call_target="tpu_custom_call" | custom-call | flops 2453667840 | bytes 10485760 | tf_op jit(solution)/shard_map/weights/pallas_call | solution.py:628
  299.8 12.3 %end.1 = (bf16[5,200,768]{2,1,0:T(8,128)(2,1)}, f32[8,768]{1,0:T(8,128)S(1)}) custom-call(s32[2]{0:T(128)S(1)} %copy-done.7, bf16[1040,384]{1,0:T(8,128)(2,1)S(1)} %get-tuple-element.126.qa.grad_q, bf16[1040,384]{1,0:T(8,128)(2,1)S(1)} %get-tuple-element.127.ka.grad_k, bf16[1040,384]{1,0:T(8,128)(2,1)S(1)} %get-tuple-element.128.va.grad_v, ...), custom_call_target="tpu_custom_call" | custom-call | flops 3680501760 | bytes 20971520 | tf_op jit(solution)/shard_map/end/pallas_call | solution.py:665
  312.3 8.8 %table.1 = f32[12,768]{1,0:T(8,128)S(1)} custom-call(s32[208,1]{1,0:T(8,128)S(1)} %copy.80.spots_down, s32[1,208]{1,0:T(1,128)S(1)} %bitcast.198, s32[208,8]{1,0:T(8,128)S(1)} %pad.30.edge_rows, f32[6,208,208]{2,1,0:T(8,128)S(1)} %copy-done.33, f32[6,208,208]{2,1,0:T(8,128)S(1)} %copy-done.32), custom_call_target="tpu_custom_call" | custom-call | flops 1472200704 | bytes 2076672 | tf_op jit(solution)/shard_map/table/pallas_call | solution.py:229
  322.4 4.5 %collective-permute-done.21 = f32[16128]{0:T(1024)S(1)} collective-permute-done((f32[16128]{0:T(1024)S(1)}, f32[16128]{0:T(1024)S(1)}, u32[]{:S(2)}, u32[]{:S(2)}) %collective-permute-start.21) | collective-permute-done | bytes 64544 | tf_op jit(solution)/shard_map/ppermute | solution.py:724
  327.2 5.6 %collective-permute-start.22 = (f32[11520]{0:T(1024)S(1)}, f32[11520]{0:T(1024)S(1)}, u32[]{:S(2)}, u32[]{:S(2)}) collective-permute-start(f32[11520]{0:T(1024)S(1)} %pad_maximum_fusion.22), channel_id=1, source_target_pairs={{0,2},{1,3},{2,0},{3,1},{4,6},{5,7},{6,4},{7,5},{8,10},{9,11},{10,... | collective-permute-start | bytes 138248 | tf_op jit(solution)/shard_map/ppermute | solution.py:724
  350.7 8.5 %collective-permute-done.30 = bf16[2,2,12,16,384]{4,3,2,1,0:T(8,128)(2,1)S(1)} collective-permute-done((bf16[2,2,12,16,384]{4,3,2,1,0:T(8,128)(2,1)S(1)}, bf16[2,2,12,16,384]{4,3,2,1,0:T(8,128)(2,1)S(1)}, u32[]{:S(2)}, u32[]{:S(2)}) %collective-permute-start.30) | collective-permute-done | bytes 589856 | tf_op jit(solution)/shard_map/ppermute | solution.py:724
  360.0 5.1 %collective-permute-done.27 = bf16[2,2,12,16,384]{4,3,2,1,0:T(8,128)(2,1)S(1)} collective-permute-done((bf16[2,2,12,16,384]{4,3,2,1,0:T(8,128)(2,1)S(1)}, bf16[2,2,12,16,384]{4,3,2,1,0:T(8,128)(2,1)S(1)}, u32[]{:S(2)}, u32[]{:S(2)}) %collective-permute-start.27) | collective-permute-done | bytes 589856 | tf_op jit(solution)/shard_map/ppermute | solution.py:724
  381.1 16.2 %collective-permute-done.41 = bf16[2,4,96,768]{3,2,1,0:T(8,128)(2,1)S(1)} collective-permute-done((bf16[2,4,96,768]{3,2,1,0:T(8,128)(2,1)S(1)}, bf16[2,4,96,768]{3,2,1,0:T(8,128)(2,1)S(1)}, u32[]{:S(2)}, u32[]{:S(2)}) %collective-permute-start.41) | collective-permute-done | bytes 1179680 | tf_op jit(solution)/shard_map/ppermute | solution.py:724
  399.2 6.0 %collective-permute-done.38 = bf16[2,4,96,768]{3,2,1,0:T(8,128)(2,1)S(1)} collective-permute-done((bf16[2,4,96,768]{3,2,1,0:T(8,128)(2,1)S(1)}, bf16[2,4,96,768]{3,2,1,0:T(8,128)(2,1)S(1)}, u32[]{:S(2)}, u32[]{:S(2)}) %collective-permute-start.38) | collective-permute-done | bytes 1179680 | tf_op jit(solution)/shard_map/ppermute | solution.py:724
  409.2 4.7 %collective-permute-done.42 = bf16[4,96,768]{2,1,0:T(8,128)(2,1)S(1)} collective-permute-done((bf16[4,96,768]{2,1,0:T(8,128)(2,1)}, bf16[4,96,768]{2,1,0:T(8,128)(2,1)S(1)}, u32[]{:S(2)}, u32[]{:S(2)}) %collective-permute-start.42) | collective-permute-done | bytes 589856 | tf_op jit(solution)/shard_map/ppermute | solution.py:724
  420.4 4.9 %collective-permute-done.35 = bf16[2,12,16,384]{3,2,1,0:T(8,128)(2,1)S(1)} collective-permute-done((bf16[2,12,16,384]{3,2,1,0:T(8,128)(2,1)S(1)}, bf16[2,12,16,384]{3,2,1,0:T(8,128)(2,1)S(1)}, u32[]{:S(2)}, u32[]{:S(2)}) %collective-permute-start.35) | collective-permute-done | bytes 294944 | tf_op jit(solution)/shard_map/ppermute | solution.py:724
  436.8 5.8 %collective-permute-done.44 = bf16[2,96,768]{2,1,0:T(8,128)(2,1)S(1)} collective-permute-done((bf16[2,96,768]{2,1,0:T(8,128)(2,1)S(1)}, bf16[2,96,768]{2,1,0:T(8,128)(2,1)S(1)}, u32[]{:S(2)}, u32[]{:S(2)}) %collective-permute-start.44) | collective-permute-done | bytes 294944 | tf_op jit(solution)/shard_map/ppermute | solution.py:724
  (363 shorter events, 136.6 us)
Async XLA Ops:
  1.8 17.4 %collective-permute-start = (bf16[2,96,768]{2,1,0:T(8,128)(2,1)S(1)}, bf16[2,96,768]{2,1,0:T(8,128)(2,1)S(1)}, u32[]{:S(2)}, u32[]{:S(2)}) collective-permute-start(bf16[2,96,768]{2,1,0:T(8,128)(2,1)S(1)} %bitcast.207), channel_id=1, source_target_pairs={{0,2},{1,3},{2,0},{3,1},{4,6},{5,7},{6,4},{7,5},{8,10},{9,11},{10,... | collective-permute-start | bytes 884744 | tf_op jit(solution)/shard_map/ppermute | solution.py:724
  19.3 18.3 %collective-permute-start.1 = (bf16[2,2,96,768]{3,2,1,0:T(8,128)(2,1)S(1)}, bf16[2,2,96,768]{3,2,1,0:T(8,128)(2,1)S(1)}, u32[]{:S(2)}, u32[]{:S(2)}) collective-permute-start(bf16[2,2,96,768]{3,2,1,0:T(8,128)(2,1)S(1)} %get-tuple-element.231), channel_id=1, source_target_pairs={{0,1},{1,0},{2,3},{3,2},{4,5},{5,4},{6,7},{7,6},{8,9},{9,8},{10,11... | collective-permute-start | bytes 1769480 | tf_op jit(solution)/shard_map/ppermute | solution.py:724
  20.3 35.4 %collective-permute-start.5 = (f32[8,768]{1,0:T(8,128)S(1)}, f32[8,768]{1,0:T(8,128)S(1)}, u32[]{:S(2)}, u32[]{:S(2)}) collective-permute-start(f32[8,768]{1,0:T(8,128)S(1)} %scatter.14), channel_id=1, source_target_pairs={{0,2},{1,3},{2,0},{3,1},{4,6},{5,7},{6,4},{7,5},{8,10},{9,11},{10,... | collective-permute-start | bytes 73736 | tf_op jit(solution)/shard_map/ppermute | solution.py:724
  23.8 30.9 %collective-permute-start.10 = (bf16[12,16,384]{2,1,0:T(8,128)(2,1)S(1)}, bf16[12,16,384]{2,1,0:T(8,128)(2,1)S(1)}, u32[]{:S(2)}, u32[]{:S(2)}) collective-permute-start(bf16[12,16,384]{2,1,0:T(8,128)(2,1)S(1)} %constant_dynamic-slice_fusion), channel_id=1, source_target_pairs={{0,2},{1,3},{2,0},{3,1},{4,6},{5,7},{6,4},{7,5},{8,10},{9,11},{10,... | collective-permute-start | bytes 442376 | tf_op jit(solution)/shard_map/ppermute | solution.py:724
  38.9 13.6 %collective-permute-start.18 = (bf16[4,96,768]{2,1,0:T(8,128)(2,1)S(1)}, bf16[4,96,768]{2,1,0:T(8,128)(2,1)S(1)}, u32[]{:S(2)}, u32[]{:S(2)}) collective-permute-start(bf16[4,96,768]{2,1,0:T(8,128)(2,1)S(1)} %get-tuple-element.221), channel_id=1, source_target_pairs={{0,16},{1,17},{2,18},{3,19},{4,20},{5,21},{6,22},{7,23},{8,24},{9,... | collective-permute-start | bytes 1769480 | tf_op jit(solution)/shard_map/ppermute | solution.py:724
  53.7 55.1 %collective-permute-start.19 = (bf16[2,4,96,768]{3,2,1,0:T(8,128)(2,1)}, bf16[2,4,96,768]{3,2,1,0:T(8,128)(2,1)}, u32[]{:S(2)}, u32[]{:S(2)}) collective-permute-start(bf16[2,4,96,768]{3,2,1,0:T(8,128)(2,1)} %get-tuple-element.217), channel_id=1, source_target_pairs={{0,8},{1,9},{2,10},{3,11},{4,12},{5,13},{6,14},{7,15},{8,0},{9,1},... | collective-permute-start | bytes 3538952 | tf_op jit(solution)/shard_map/ppermute | solution.py:724
  55.6 17.9 %collective-permute-start.14 = (bf16[2,12,16,384]{3,2,1,0:T(8,128)(2,1)}, bf16[2,12,16,384]{3,2,1,0:T(8,128)(2,1)}, u32[]{:S(2)}, u32[]{:S(2)}) collective-permute-start(bf16[2,12,16,384]{3,2,1,0:T(8,128)(2,1)} %get-tuple-element.235), channel_id=1, source_target_pairs={{0,1},{1,0},{2,3},{3,2},{4,5},{5,4},{6,7},{7,6},{8,9},{9,8},{10,11... | collective-permute-start | bytes 884744 | tf_op jit(solution)/shard_map/ppermute | solution.py:724
  57.6 15.1 %collective-permute-start.6 = (f32[2,8,768]{2,1,0:T(8,128)}, f32[2,8,768]{2,1,0:T(8,128)}, u32[]{:S(2)}, u32[]{:S(2)}) collective-permute-start(f32[2,8,768]{2,1,0:T(8,128)} %get-tuple-element.240), channel_id=1, source_target_pairs={{0,1},{1,0},{2,3},{3,2},{4,5},{5,4},{6,7},{7,6},{8,9},{9,8},{10,11... | collective-permute-start | bytes 147464 | tf_op jit(solution)/shard_map/ppermute | solution.py:724
  70.6 16.2 %collective-permute-start.11 = (bf16[2,12,16,384]{3,2,1,0:T(8,128)(2,1)}, bf16[2,12,16,384]{3,2,1,0:T(8,128)(2,1)}, u32[]{:S(2)}, u32[]{:S(2)}) collective-permute-start(bf16[2,12,16,384]{3,2,1,0:T(8,128)(2,1)} %get-tuple-element.235), channel_id=1, source_target_pairs={{0,16},{1,17},{2,18},{3,19},{4,20},{5,21},{6,22},{7,23},{8,24},{9,... | collective-permute-start | bytes 884744 | tf_op jit(solution)/shard_map/ppermute | solution.py:724
  72.2 33.0 %collective-permute-start.2 = (bf16[4,96,768]{2,1,0:T(8,128)(2,1)}, bf16[4,96,768]{2,1,0:T(8,128)(2,1)}, u32[]{:S(2)}, u32[]{:S(2)}) collective-permute-start(bf16[4,96,768]{2,1,0:T(8,128)(2,1)} %get-tuple-element.220), channel_id=1, source_target_pairs={{0,8},{1,9},{2,10},{3,11},{4,12},{5,13},{6,14},{7,15},{8,0},{9,1},... | collective-permute-start | bytes 1769480 | tf_op jit(solution)/shard_map/ppermute | solution.py:724
  73.5 28.5 %collective-permute-start.15 = (bf16[2,12,16,384]{3,2,1,0:T(8,128)(2,1)}, bf16[2,12,16,384]{3,2,1,0:T(8,128)(2,1)}, u32[]{:S(2)}, u32[]{:S(2)}) collective-permute-start(bf16[2,12,16,384]{3,2,1,0:T(8,128)(2,1)} %collective-permute-done.14), channel_id=1, source_target_pairs={{0,8},{1,9},{2,10},{3,11},{4,12},{5,13},{6,14},{7,15},{8,0},{9,1},... | collective-permute-start | bytes 884744 | tf_op jit(solution)/shard_map/ppermute | solution.py:724
  77.8 45.5 %collective-permute-start.7 = (f32[4,96]{1,0:T(4,128)}, f32[4,96]{1,0:T(4,128)}, u32[]{:S(2)}, u32[]{:S(2)}) collective-permute-start(f32[4,96]{1,0:T(4,128)} %bitcast.25), channel_id=1, source_target_pairs={{0,16},{1,17},{2,18},{3,19},{4,20},{5,21},{6,22},{7,23},{8,24},{9,... | collective-permute-start | bytes 4616 | tf_op jit(solution)/shard_map/ppermute | solution.py:724
  88.0 25.0 %collective-permute-start.12 = (bf16[2,2,12,16,384]{4,3,2,1,0:T(8,128)(2,1)S(1)}, bf16[2,2,12,16,384]{4,3,2,1,0:T(8,128)(2,1)S(1)}, u32[]{:S(2)}, u32[]{:S(2)}) collective-permute-start(bf16[2,2,12,16,384]{4,3,2,1,0:T(8,128)(2,1)S(1)} %get-tuple-element.229), channel_id=1, source_target_pairs={{0,8},{1,9},{2,10},{3,11},{4,12},{5,13},{6,14},{7,15},{8,0},{9,1},... | collective-permute-start | bytes 1769480 | tf_op jit(solution)/shard_map/ppermute | solution.py:724
  104.2 16.6 %collective-permute-start.16 = (bf16[2,2,12,16,384]{4,3,2,1,0:T(8,128)(2,1)}, bf16[2,2,12,16,384]{4,3,2,1,0:T(8,128)(2,1)}, u32[]{:S(2)}, u32[]{:S(2)}) collective-permute-start(bf16[2,2,12,16,384]{4,3,2,1,0:T(8,128)(2,1)} %get-tuple-element.227), channel_id=1, source_target_pairs={{0,16},{1,17},{2,18},{3,19},{4,20},{5,21},{6,22},{7,23},{8,24},{9,... | collective-permute-start | bytes 1769480 | tf_op jit(solution)/shard_map/ppermute | solution.py:724
  107.8 30.1 %collective-permute-start.3 = (bf16[2,4,96,768]{3,2,1,0:T(8,128)(2,1)}, bf16[2,4,96,768]{3,2,1,0:T(8,128)(2,1)}, u32[]{:S(2)}, u32[]{:S(2)}) collective-permute-start(bf16[2,4,96,768]{3,2,1,0:T(8,128)(2,1)} %get-tuple-element.223), channel_id=1, source_target_pairs={{0,16},{1,17},{2,18},{3,19},{4,20},{5,21},{6,22},{7,23},{8,24},{9,... | collective-permute-start | bytes 3538952 | tf_op jit(solution)/shard_map/ppermute | solution.py:724
  111.7 77.1 %collective-permute-start.20 = (bf16[16,96,768]{2,1,0:T(8,128)(2,1)}, bf16[16,96,768]{2,1,0:T(8,128)(2,1)}, u32[]{:S(2)}, u32[]{:S(2)}) collective-permute-start(bf16[16,96,768]{2,1,0:T(8,128)(2,1)} %bitcast.63.up_m.down_m), channel_id=1, source_target_pairs={{0,4},{1,5},{2,6},{3,7},{4,0},{5,1},{6,2},{7,3},{8,12},{9,13},{10,... | collective-permute-start | bytes 7077896 | tf_op jit(solution)/shard_map/ppermute | solution.py:724
  114.1 35.7 %collective-permute-start.13 = (bf16[4,2,12,16,384]{4,3,2,1,0:T(8,128)(2,1)}, bf16[4,2,12,16,384]{4,3,2,1,0:T(8,128)(2,1)}, u32[]{:S(2)}, u32[]{:S(2)}) collective-permute-start(bf16[4,2,12,16,384]{4,3,2,1,0:T(8,128)(2,1)} %bitcast.42.mine), channel_id=1, source_target_pairs={{0,4},{1,5},{2,6},{3,7},{4,0},{5,1},{6,2},{7,3},{8,12},{9,13},{10,... | collective-permute-start | bytes 3538952 | tf_op jit(solution)/shard_map/ppermute | solution.py:724
  123.3 42.8 %collective-permute-start.17 = (bf16[4,2,12,16,384]{4,3,2,1,0:T(8,128)(2,1)}, bf16[4,2,12,16,384]{4,3,2,1,0:T(8,128)(2,1)}, u32[]{:S(2)}, u32[]{:S(2)}) collective-permute-start(bf16[4,2,12,16,384]{4,3,2,1,0:T(8,128)(2,1)} %bitcast.55.mine), channel_id=1, source_target_pairs={{0,4},{1,5},{2,6},{3,7},{4,0},{5,1},{6,2},{7,3},{8,12},{9,13},{10,... | collective-permute-start | bytes 3538952 | tf_op jit(solution)/shard_map/ppermute | solution.py:724
  128.2 16.8 %collective-permute-start.9 = (f32[2,2,4,96]{3,2,0,1:T(4,128)}, f32[2,2,4,96]{3,2,0,1:T(4,128)}, u32[]{:S(2)}, u32[]{:S(2)}) collective-permute-start(f32[2,2,4,96]{3,2,0,1:T(4,128)} %get-tuple-element.254), channel_id=1, source_target_pairs={{0,4},{1,5},{2,6},{3,7},{4,0},{5,1},{6,2},{7,3},{8,12},{9,13},{10,... | collective-permute-start | bytes 18440 | tf_op jit(solution)/shard_map/ppermute | solution.py:724
  140.9 80.1 %collective-permute-start.4 = (bf16[16,96,768]{2,1,0:T(8,128)(2,1)}, bf16[16,96,768]{2,1,0:T(8,128)(2,1)}, u32[]{:S(2)}, u32[]{:S(2)}) collective-permute-start(bf16[16,96,768]{2,1,0:T(8,128)(2,1)} %bitcast.17.up_m.down_m), channel_id=1, source_target_pairs={{0,4},{1,5},{2,6},{3,7},{4,0},{5,1},{6,2},{7,3},{8,12},{9,13},{10,... | collective-permute-start | bytes 7077896 | tf_op jit(solution)/shard_map/ppermute | solution.py:724
  341.6 28.4 %collective-permute-start.40 = (bf16[16,96,768]{2,1,0:T(8,128)(2,1)}, bf16[16,96,768]{2,1,0:T(8,128)(2,1)}, u32[]{:S(2)}, u32[]{:S(2)}) collective-permute-start(bf16[16,96,768]{2,1,0:T(8,128)(2,1)} %get-tuple-element.155), channel_id=1, source_target_pairs={{0,4},{1,5},{2,6},{3,7},{4,0},{5,1},{6,2},{7,3},{8,12},{9,13},{10,... | collective-permute-start | bytes 7077896 | tf_op jit(solution)/shard_map/ppermute | solution.py:724
  341.6 31.5 %collective-permute-start.37 = (bf16[16,96,768]{2,1,0:T(8,128)(2,1)}, bf16[16,96,768]{2,1,0:T(8,128)(2,1)}, u32[]{:S(2)}, u32[]{:S(2)}) collective-permute-start(bf16[16,96,768]{2,1,0:T(8,128)(2,1)} %get-tuple-element.153), channel_id=1, source_target_pairs={{0,4},{1,5},{2,6},{3,7},{4,0},{5,1},{6,2},{7,3},{8,12},{9,13},{10,... | collective-permute-start | bytes 7077896 | tf_op jit(solution)/shard_map/ppermute | solution.py:724
  345.9 13.3 %collective-permute-start.30 = (bf16[2,2,12,16,384]{4,3,2,1,0:T(8,128)(2,1)S(1)}, bf16[2,2,12,16,384]{4,3,2,1,0:T(8,128)(2,1)S(1)}, u32[]{:S(2)}, u32[]{:S(2)}) collective-permute-start(bf16[2,2,12,16,384]{4,3,2,1,0:T(8,128)(2,1)S(1)} %slice.394), channel_id=1, source_target_pairs={{0,16},{1,17},{2,18},{3,19},{4,20},{5,21},{6,22},{7,23},{8,24},{9,... | collective-permute-start | bytes 1769480 | tf_op jit(solution)/shard_map/ppermute | solution.py:724
  349.1 16.0 %collective-permute-start.27 = (bf16[2,2,12,16,384]{4,3,2,1,0:T(8,128)(2,1)S(1)}, bf16[2,2,12,16,384]{4,3,2,1,0:T(8,128)(2,1)S(1)}, u32[]{:S(2)}, u32[]{:S(2)}) collective-permute-start(bf16[2,2,12,16,384]{4,3,2,1,0:T(8,128)(2,1)S(1)} %slice.390), channel_id=1, source_target_pairs={{0,8},{1,9},{2,10},{3,11},{4,12},{5,13},{6,14},{7,15},{8,0},{9,1},... | collective-permute-start | bytes 1769480 | tf_op jit(solution)/shard_map/ppermute | solution.py:724
  365.3 11.8 %collective-permute-start.28 = (bf16[2,12,16,384]{3,2,1,0:T(8,128)(2,1)S(1)}, bf16[2,12,16,384]{3,2,1,0:T(8,128)(2,1)S(1)}, u32[]{:S(2)}, u32[]{:S(2)}) collective-permute-start(bf16[2,12,16,384]{3,2,1,0:T(8,128)(2,1)S(1)} %slice_bitcast_fusion.12), channel_id=1, source_target_pairs={{0,16},{1,17},{2,18},{3,19},{4,20},{5,21},{6,22},{7,23},{8,24},{9,... | collective-permute-start | bytes 884744 | tf_op jit(solution)/shard_map/ppermute | solution.py:724
  372.5 24.9 %collective-permute-start.41 = (bf16[2,4,96,768]{3,2,1,0:T(8,128)(2,1)S(1)}, bf16[2,4,96,768]{3,2,1,0:T(8,128)(2,1)S(1)}, u32[]{:S(2)}, u32[]{:S(2)}) collective-permute-start(bf16[2,4,96,768]{3,2,1,0:T(8,128)(2,1)S(1)} %bitcast.209), channel_id=1, source_target_pairs={{0,16},{1,17},{2,18},{3,19},{4,20},{5,21},{6,22},{7,23},{8,24},{9,... | collective-permute-start | bytes 3538952 | tf_op jit(solution)/shard_map/ppermute | solution.py:724
  376.5 28.7 %collective-permute-start.38 = (bf16[2,4,96,768]{3,2,1,0:T(8,128)(2,1)S(1)}, bf16[2,4,96,768]{3,2,1,0:T(8,128)(2,1)S(1)}, u32[]{:S(2)}, u32[]{:S(2)}) collective-permute-start(bf16[2,4,96,768]{3,2,1,0:T(8,128)(2,1)S(1)} %bitcast.210), channel_id=1, source_target_pairs={{0,8},{1,9},{2,10},{3,11},{4,12},{5,13},{6,14},{7,15},{8,0},{9,1},... | collective-permute-start | bytes 3538952 | tf_op jit(solution)/shard_map/ppermute | solution.py:724
  377.1 29.9 %collective-permute-start.25 = (f32[10848]{0:T(1024)S(1)}, f32[10848]{0:T(1024)S(1)}, u32[]{:S(2)}, u32[]{:S(2)}) collective-permute-start(f32[10848]{0:T(1024)S(1)} %pad_maximum_fusion.25), channel_id=1, source_target_pairs={{0,4},{1,5},{2,6},{3,7},{4,0},{5,1},{6,2},{7,3},{8,12},{9,13},{10,... | collective-permute-start | bytes 130184 | tf_op jit(solution)/shard_map/ppermute | solution.py:724
  377.9 29.8 %collective-permute-start.33 = (bf16[12,16,384]{2,1,0:T(8,128)(2,1)}, bf16[12,16,384]{2,1,0:T(8,128)(2,1)S(1)}, u32[]{:S(2)}, u32[]{:S(2)}) collective-permute-start(bf16[12,16,384]{2,1,0:T(8,128)(2,1)} %slice_bitcast_fusion.14), channel_id=1, source_target_pairs={{0,2},{1,3},{2,0},{3,1},{4,6},{5,7},{6,4},{7,5},{8,10},{9,11},{10,... | collective-permute-start | bytes 442376 | tf_op jit(solution)/shard_map/ppermute | solution.py:724
  398.5 15.4 %collective-permute-start.42 = (bf16[4,96,768]{2,1,0:T(8,128)(2,1)}, bf16[4,96,768]{2,1,0:T(8,128)(2,1)S(1)}, u32[]{:S(2)}, u32[]{:S(2)}) collective-permute-start(bf16[4,96,768]{2,1,0:T(8,128)(2,1)} %slice_bitcast_fusion), channel_id=1, source_target_pairs={{0,8},{1,9},{2,10},{3,11},{4,12},{5,13},{6,14},{7,15},{8,0},{9,1},... | collective-permute-start | bytes 1769480 | tf_op jit(solution)/shard_map/ppermute | solution.py:724
  407.8 10.6 %collective-permute-start.34 = (bf16[12,16,384]{2,1,0:T(8,128)(2,1)S(1)}, bf16[12,16,384]{2,1,0:T(8,128)(2,1)S(1)}, u32[]{:S(2)}, u32[]{:S(2)}) collective-permute-start(bf16[12,16,384]{2,1,0:T(8,128)(2,1)S(1)} %fusion.11), channel_id=1, source_target_pairs={{0,16},{1,17},{2,18},{3,19},{4,20},{5,21},{6,22},{7,23},{8,24},{9,... | collective-permute-start | bytes 442376 | tf_op jit(solution)/shard_map/ppermute | solution.py:724
  428.0 14.6 %collective-permute-start.44 = (bf16[2,96,768]{2,1,0:T(8,128)(2,1)S(1)}, bf16[2,96,768]{2,1,0:T(8,128)(2,1)S(1)}, u32[]{:S(2)}, u32[]{:S(2)}) collective-permute-start(bf16[2,96,768]{2,1,0:T(8,128)(2,1)S(1)} %slice_bitcast_fusion.8), channel_id=1, source_target_pairs={{0,2},{1,3},{2,0},{3,1},{4,6},{5,7},{6,4},{7,5},{8,10},{9,11},{10,... | collective-permute-start | bytes 884744 | tf_op jit(solution)/shard_map/ppermute | solution.py:724
  (74 other events, 681.0 us)
